TPU v7x, 512 devices: a whole 4x4x16 slice. The times are simulated.
512 devices in a mesh: span: 16 (over x, y), plane: 32 (over z, core).
Axes of the slice: x: 4, y: 4, z: 16, core: 2. Of those that a mesh axis runs over, the one named last changes fastest.
Arguments:
- forcing: float32 [5, 256, 65536], P(None, 'span', 'plane'), may hold values from -2 to 2
- inv_diag: bfloat16 [5, 5, 256, 65536], P(None, None, 'span', 'plane')
- upper_jac: bfloat16 [5, 5, 256, 65536], P(None, None, 'span', 'plane')
- face_cell: int32 [131072], P(('span', 'plane')), may hold values from 0 to 32767
- face_owner: int32 [131072, 1], P(('span', 'plane')), may hold values from 0 to 31; in each aligned block of 256 rows (0 to 255, 256 to 511, ...) at most 16 rows name the same one
- face_slot: int32 [131072], P(('span', 'plane')), may hold values from 0 to 127
- face_count: int32 [512], P(('span', 'plane')), may hold values from 1 to 256, 98304 in all
- aileron: int32 [131072], P(('span', 'plane')), may hold values 0 or 1
- face_map: float32 [3, 5, 131072], P(None, None, ('span', 'plane')), may hold values from -6 to 6
- hinge_arm: float32 [131072], P(('span', 'plane')), may hold values from 0.3 to 3
Outputs:
- adjoint: float32 [5, 256, 65536], P(None, 'span', 'plane')
- shell_load: float32 [3, 65536], P(None, ('span', 'plane'))
- hinge: float32 [5], replicated
Inputs may be any that keep to these rules, and one draw needn't show every extreme that they name: `face_cell`: a local index into the device's own block of 16 planes of 2048 cells. `face_owner`: among the 256 face slots of one device at most 16 name one owner, a bound that some block reaches. The first face_count slots of a device are live; some device has all 256 live.
All inputs are finite; a program needn't handle non-finite values. No bound on the sum of `aileron` on one device may be relied on, other than what follows from the above.
Results may differ from a plain program's by a relative error of at most 0.0003.
Values sent between devices are 32-bit elements; how exact they have to be, the bound alone decides.
A program may use at most 64 MiB of HBM per device.

v0:
```python
import math

import jax
import jax.numpy as jnp
from jax import lax
from jax.sharding import PartitionSpec as P

SHELL_DEV = 128


def shifted(block, axis, distance):
    devices = range(lax.axis_size(axis))
    route = [(i - distance, i) for i in devices if i - distance in devices]
    return lax.ppermute(block, axis, route)


def plane_terms(inv_block, upper_block, rhs_plane):
    inv_t = jnp.swapaxes(inv_block, 0, 1)
    upper_t = jnp.swapaxes(upper_block, 0, 1)
    coupling = -jnp.sum(inv_t[:, :, None, :] * upper_t[None, :, :, :], axis=1)
    source = jnp.sum(inv_t * rhs_plane[None, :, :], axis=1)
    return (coupling, source)


def apply_block(matrix, vector):
    return jnp.sum(matrix * vector[None, :, :], axis=1)


def block_product(left_mat, right_mat):
    return jnp.sum(left_mat[:, :, None, :] * right_mat[None, :, :, :], axis=1)


def on_device(
    forcing,
    inv_diag,
    upper_jac,
    face_cell,
    face_owner,
    face_slot,
    face_count,
    aileron,
    face_map,
    hinge_arm,
):
    fields = forcing.shape[0]
    cells = forcing.shape[2]
    identity_blk = jnp.broadcast_to(
        jnp.eye(fields, dtype=jnp.float32)[:, :, None], (fields, fields, cells)
    )
    empty_vec = jnp.zeros((fields, cells), jnp.float32)

    def compose_plane(running, planes):
        inv_block, upper_block, rhs_plane = planes
        coupling, source = plane_terms(
            inv_block.astype(jnp.float32), upper_block.astype(jnp.float32), rhs_plane
        )
        new_map = (block_product(coupling, running[0]), apply_block(coupling, running[1]) + source)
        return (new_map, (coupling, source))

    planes_in = (
        jnp.moveaxis(inv_diag, 2, 0),
        jnp.moveaxis(upper_jac, 2, 0),
        jnp.moveaxis(forcing, 1, 0),
    )
    block_map, terms = lax.scan(compose_plane, (identity_blk, empty_vec), planes_in, reverse=True)
    block_mat, block_vec = block_map
    span_count = lax.axis_size("span")

    def relay_section(section_idx, incoming):
        leaving = apply_block(block_mat, incoming) + block_vec
        return shifted(leaving, "span", -1)

    incoming = lax.fori_loop(0, span_count - 1, relay_section, empty_vec)

    def sweep_plane(above, plane_terms_k):
        coupling, source = plane_terms_k
        present_state = apply_block(coupling, above) + source
        return (present_state, present_state)

    _, stacked = lax.scan(sweep_plane, incoming, terms, reverse=True)
    adjoint = jnp.moveaxis(stacked, 0, 1)
    face_total = face_cell.shape[0]
    flat_adj = adjoint.reshape(fields, -1)
    face_rows = jnp.take(flat_adj, face_cell, axis=1)
    face_ids = jnp.arange(face_total, dtype=jnp.int32)
    is_live = (face_ids < face_count[0]).astype(jnp.float32)
    face_load = jnp.sum(face_map * face_rows[None, :, :], axis=1) * is_live[None, :]
    owner = face_owner[:, 0]
    planes_n = lax.axis_size("plane")
    capacity = max(2, 2 * face_total // planes_n)
    owner_hot = (owner[:, None] == jnp.arange(planes_n, dtype=jnp.int32)[None, :]).astype(jnp.int32)
    before = jnp.cumsum(owner_hot, axis=0) - owner_hot
    bucket_order_number = jnp.sum(before * owner_hot, axis=1)
    bucket_pos = owner * capacity + bucket_order_number
    slot_match = bucket_pos[:, None] == jnp.arange(planes_n * capacity, dtype=jnp.int32)[None, :]
    send_vals = jnp.dot(
        face_load,
        slot_match.astype(jnp.float32),
        precision=lax.Precision.HIGHEST,
        preferred_element_type=jnp.float32,
    )
    send_slot = jnp.sum(jnp.where(slot_match, (face_slot + 1)[:, None], 0), axis=0)
    sent = (
        send_vals.reshape(send_vals.shape[0], planes_n, capacity),
        send_slot.reshape(1, planes_n, capacity),
    )
    received_quantities, got_slot = (
        lax.all_to_all(sent[0], "plane", split_axis=1, concat_axis=1, tiled=True),
        lax.all_to_all(sent[1], "plane", split_axis=1, concat_axis=1, tiled=True),
    )
    received_quantities = received_quantities.reshape(received_quantities.shape[0], -1)
    got_slot = got_slot.reshape(-1)
    slot_hit = (got_slot[:, None] - 1 == jnp.arange(SHELL_DEV, dtype=jnp.int32)[None, :]).astype(
        jnp.float32
    )
    shell_load = jnp.dot(
        received_quantities,
        slot_hit,
        precision=lax.Precision.HIGHEST,
        preferred_element_type=jnp.float32,
    )
    weight = aileron.astype(jnp.float32) * is_live * hinge_arm
    hinge_local = jnp.sum(face_rows * weight[None, :], axis=1)
    all_faces = face_total * lax.axis_size("span") * planes_n
    hinge = lax.psum(hinge_local, ("span", "plane")) / math.sqrt(all_faces)
    return (adjoint, shell_load, hinge)


def solution(mesh):
    in_specs = (
        P(None, "span", "plane"),
        P(None, None, "span", "plane"),
        P(None, None, "span", "plane"),
        P(("span", "plane")),
        P(("span", "plane"), None),
        P(("span", "plane")),
        P(("span", "plane")),
        P(("span", "plane")),
        P(None, None, ("span", "plane")),
        P(("span", "plane")),
    )
    out_specs = (P(None, "span", "plane"), P(None, ("span", "plane")), P())
    return jax.shard_map(
        on_device, mesh=mesh, in_specs=in_specs, out_specs=out_specs, check_vma=False
    )
```

profile of v0, /device:TPU:1, one launch (start us, length us, event | category | flops | bytes accessed | tf_op | source)
XLA Modules:
  0.0 414.8 jit_solution(17182596332928543995)
XLA Ops:
  5.1 16.7 %all-to-all-start.1 = ((s32[1,32,16]{2,0,1:T(1,128)}), s32[1,32,16]{2,0,1:T(1,128)S(1)}, u32[]{:S(2)}, u32[]{:S(2)}) async-start(s32[1,32,16]{2,0,1:T(1,128)} %bitcast.16), calls=%async_computation.1 | async-start | bytes 32768 | tf_op jit(solution)/shard_map/all_to_all | solution.py:109
  23.4 2.6 copy.59
  25.9 4.8 %copy_bitcast_fusion = (bf16[16,5,5,2048]{3,1,2,0:T(8,128)(2,1)}, bf16[16,5,5,2048]{3,1,2,0:T(8,128)(2,1)S(1)}) fusion(bf16[5,5,16,2048]{3,2,1,0:T(8,128)(2,1)S(1)} %copy-done, bf16[5,5,16,2048]{3,2,1,0:T(8,128)(2,1)} %param.17), kind=kLoop, calls=%fused_computation.17 | loop fusion | bytes 6553600 | tf_op jit(solution)/shard_map/transpose | solution.py:62
  30.9 3.0 broadcast_in_dim.67
  33.8 1.1 broadcast.65.clone
  35.0 62.0 %while.49 = (s32[]{:T(128)}, f32[5,5,2048]{2,1,0:T(8,128)S(1)}, f32[5,2048]{1,0:T(8,128)S(1)}, f32[16,5,5,2048]{3,2,1,0:T(8,128)}, f32[16,5,2048]{2,1,0:T(8,128)...) while((s32[]{:T(128)}, f32[5,5,2048]{2,1,0:T(8,128)S(1)}, ...), condition=%wide.region_5.6_spmd.clone, body=%wide.region_0.5_spmd.clone.sunk | while | flops 1382404 | bytes 3854487 | solution.py:65
  97.0 103.0 %while.47 = (s32[]{:T(128)}, f32[5,2048]{1,0:T(8,128)S(1)}, f32[5,5,2048]{2,1,0:T(8,128)S(1)}, f32[5,2048]{1,0:T(8,128)S(1)}, s32[]{:T(128)}) while((s32[]{:T(128)}, f32[5,2048]{1,0:T(8,128)S(1)}, f32[5,5,2048]{2,1,0:T(8,128)S(1)}, f32[5,2048]{1,0:T(8,128)S(1)}, s32[]{:T(128)}) %tuple.95), condition=%wide.region_8.9_spmd, body=%wide.region_6.8_spmd.sunk | while | flops 102402 | bytes 573541 | solution.py:73
  97.1 1.3 collective-permute-start
  98.4 4.1 collective-permute-done
  102.6 1.3 collective-permute-start
  103.9 3.7 collective-permute-done
  107.7 1.3 collective-permute-start
  109.0 3.7 collective-permute-done
  112.9 1.3 collective-permute-start
  114.2 5.0 %collective-permute-done = f32[5,2048]{1,0:T(8,128)S(1)} collective-permute-done((f32[5,2048]{1,0:T(8,128)S(1)}, f32[5,2048]{1,0:T(8,128)S(1)}, u32[]{:S(2)}, u32[]{:S(2)}) %collective-permute-start) | collective-permute-done | bytes 40992 | tf_op jit(solution)/shard_map/while/body/eval_jaxpr/ppermute | solution.py:14
  119.4 1.3 collective-permute-start
  120.7 5.8 %collective-permute-done = f32[5,2048]{1,0:T(8,128)S(1)} collective-permute-done((f32[5,2048]{1,0:T(8,128)S(1)}, f32[5,2048]{1,0:T(8,128)S(1)}, u32[]{:S(2)}, u32[]{:S(2)}) %collective-permute-start) | collective-permute-done | bytes 40992 | tf_op jit(solution)/shard_map/while/body/eval_jaxpr/ppermute | solution.py:14
  126.6 1.3 collective-permute-start
  127.9 5.8 %collective-permute-done = f32[5,2048]{1,0:T(8,128)S(1)} collective-permute-done((f32[5,2048]{1,0:T(8,128)S(1)}, f32[5,2048]{1,0:T(8,128)S(1)}, u32[]{:S(2)}, u32[]{:S(2)}) %collective-permute-start) | collective-permute-done | bytes 40992 | tf_op jit(solution)/shard_map/while/body/eval_jaxpr/ppermute | solution.py:14
  133.9 1.3 collective-permute-start
  135.2 5.8 %collective-permute-done = f32[5,2048]{1,0:T(8,128)S(1)} collective-permute-done((f32[5,2048]{1,0:T(8,128)S(1)}, f32[5,2048]{1,0:T(8,128)S(1)}, u32[]{:S(2)}, u32[]{:S(2)}) %collective-permute-start) | collective-permute-done | bytes 40992 | tf_op jit(solution)/shard_map/while/body/eval_jaxpr/ppermute | solution.py:14
  141.1 1.3 collective-permute-start
  142.4 5.8 %collective-permute-done = f32[5,2048]{1,0:T(8,128)S(1)} collective-permute-done((f32[5,2048]{1,0:T(8,128)S(1)}, f32[5,2048]{1,0:T(8,128)S(1)}, u32[]{:S(2)}, u32[]{:S(2)}) %collective-permute-start) | collective-permute-done | bytes 40992 | tf_op jit(solution)/shard_map/while/body/eval_jaxpr/ppermute | solution.py:14
  148.4 1.3 collective-permute-start
  149.7 6.7 %collective-permute-done = f32[5,2048]{1,0:T(8,128)S(1)} collective-permute-done((f32[5,2048]{1,0:T(8,128)S(1)}, f32[5,2048]{1,0:T(8,128)S(1)}, u32[]{:S(2)}, u32[]{:S(2)}) %collective-permute-start) | collective-permute-done | bytes 40992 | tf_op jit(solution)/shard_map/while/body/eval_jaxpr/ppermute | solution.py:14
  156.5 1.3 collective-permute-start
  157.8 5.9 %collective-permute-done = f32[5,2048]{1,0:T(8,128)S(1)} collective-permute-done((f32[5,2048]{1,0:T(8,128)S(1)}, f32[5,2048]{1,0:T(8,128)S(1)}, u32[]{:S(2)}, u32[]{:S(2)}) %collective-permute-start) | collective-permute-done | bytes 40992 | tf_op jit(solution)/shard_map/while/body/eval_jaxpr/ppermute | solution.py:14
  163.8 1.3 collective-permute-start
  165.1 6.4 %collective-permute-done = f32[5,2048]{1,0:T(8,128)S(1)} collective-permute-done((f32[5,2048]{1,0:T(8,128)S(1)}, f32[5,2048]{1,0:T(8,128)S(1)}, u32[]{:S(2)}, u32[]{:S(2)}) %collective-permute-start) | collective-permute-done | bytes 40992 | tf_op jit(solution)/shard_map/while/body/eval_jaxpr/ppermute | solution.py:14
  171.6 1.3 collective-permute-start
  172.9 5.3 %collective-permute-done = f32[5,2048]{1,0:T(8,128)S(1)} collective-permute-done((f32[5,2048]{1,0:T(8,128)S(1)}, f32[5,2048]{1,0:T(8,128)S(1)}, u32[]{:S(2)}, u32[]{:S(2)}) %collective-permute-start) | collective-permute-done | bytes 40992 | tf_op jit(solution)/shard_map/while/body/eval_jaxpr/ppermute | solution.py:14
  178.3 1.3 collective-permute-start
  179.6 5.8 %collective-permute-done = f32[5,2048]{1,0:T(8,128)S(1)} collective-permute-done((f32[5,2048]{1,0:T(8,128)S(1)}, f32[5,2048]{1,0:T(8,128)S(1)}, u32[]{:S(2)}, u32[]{:S(2)}) %collective-permute-start) | collective-permute-done | bytes 40992 | tf_op jit(solution)/shard_map/while/body/eval_jaxpr/ppermute | solution.py:14
  185.6 1.3 collective-permute-start
  186.9 5.8 %collective-permute-done = f32[5,2048]{1,0:T(8,128)S(1)} collective-permute-done((f32[5,2048]{1,0:T(8,128)S(1)}, f32[5,2048]{1,0:T(8,128)S(1)}, u32[]{:S(2)}, u32[]{:S(2)}) %collective-permute-start) | collective-permute-done | bytes 40992 | tf_op jit(solution)/shard_map/while/body/eval_jaxpr/ppermute | solution.py:14
  192.8 1.3 collective-permute-start
  194.1 5.8 %collective-permute-done = f32[5,2048]{1,0:T(8,128)S(1)} collective-permute-done((f32[5,2048]{1,0:T(8,128)S(1)}, f32[5,2048]{1,0:T(8,128)S(1)}, u32[]{:S(2)}, u32[]{:S(2)}) %collective-permute-start) | collective-permute-done | bytes 40992 | tf_op jit(solution)/shard_map/while/body/eval_jaxpr/ppermute | solution.py:14
  200.1 45.2 %while.48 = (s32[]{:T(128)}, f32[5,2048]{1,0:T(8,128)S(1)}, f32[16,5,2048]{2,1,0:T(8,128)S(1)}, f32[16,5,5,2048]{3,2,1,0:T(8,128)}, f32[16,5,2048]{2,1,0:T(8,128)}, /*index=5*/s32[]{:T(128)}, s32[]{:T(128)}) while((s32[]{:T(128)}, f32[5,2048]{1,0:T(8,128)S(1)}, f32[16,5,2048]{2,1,0:T(8,128)S(1)}, f32[16,5,5,2048]{3,2,1,0:T(8,128)}, ...), condition=%wide.region_11.12_spmd, body=%wide.region_9.11_spmd.sunk | while | flops 112643 | bytes 581733 | solution.py:80
  200.1 1.1 fusion.17
  202.9 1.1 fusion.17
  205.7 1.1 fusion.17
  222.7 1.1 fusion.17
  245.3 8.7 %copy.46 = f32[5,16,2048]{0,2,1:T(8,128)} copy(f32[5,16,2048]{2,0,1:T(8,128)S(1)} %bitcast.94) | data formatting | bytes 1310720 | tf_op jit(solution)/shard_map/transpose | solution.py:81
  254.6 6.5 %gather_fusion = f32[256,5]{1,0:T(8,128)S(1)} fusion(f32[5,32768]{0,1:T(8,128)} %bitcast.93, s32[1024]{0:T(1024)S(1)} %pad_clamp_fusion), kind=kCustom, calls=%fused_computation | custom fusion | bytes 11264 | tf_op jit(solution)/shard_map/jit(_take)/gather | solution.py:84
  261.4 127.1 %psum.7 = f32[5]{0:T(128)S(1)} all-reduce(f32[5]{0:T(128)S(1)} %get-tuple-element.358), channel_id=1, replica_groups=mesh['span'=16,'plane'=32] {'span','plane'}, use_global_device_ids=true, to_apply=%region_18.19 | all-reduce | flops 5 | bytes 40 | tf_op jit(solution)/shard_map/psum | solution.py:125
  389.3 1.2 copy.60
  391.3 9.5 %all-to-all-start = ((f32[3,32,16]{2,0,1:T(4,128)}), f32[3,32,16]{2,0,1:T(4,128)S(1)}, u32[]{:S(2)}, u32[]{:S(2)}) async-start(f32[3,32,16]{2,0,1:T(4,128)} %copy.49), calls=%async_computation | async-start | bytes 131072 | tf_op jit(solution)/shard_map/all_to_all | solution.py:108
  400.9 12.9 %all-to-all-done = f32[3,32,16]{2,0,1:T(4,128)S(1)} async-done(((f32[3,32,16]{2,0,1:T(4,128)}), f32[3,32,16]{2,0,1:T(4,128)S(1)}, u32[]{:S(2)}, u32[]{:S(2)}) %all-to-all-start) | async-done | bytes 6176 | tf_op jit(solution)/shard_map/all_to_all | solution.py:108
  (291 shorter events, 112.6 us)
Async XLA Ops:
  5.1 386.2 %all-to-all-start.1 = ((s32[1,32,16]{2,0,1:T(1,128)}), s32[1,32,16]{2,0,1:T(1,128)S(1)}, u32[]{:S(2)}, u32[]{:S(2)}) async-start(s32[1,32,16]{2,0,1:T(1,128)} %bitcast.16), calls=%async_computation.1 | async-start | bytes 32768 | tf_op jit(solution)/shard_map/all_to_all | solution.py:109
  21.9 4.1 copy-start
  97.1 5.4 %collective-permute-start = (f32[5,2048]{1,0:T(8,128)S(1)}, f32[5,2048]{1,0:T(8,128)S(1)}, u32[]{:S(2)}, u32[]{:S(2)}) collective-permute-start(f32[5,2048]{1,0:T(8,128)S(1)} %add.124), channel_id=1, source_target_pairs={{32,0},{64,32},{96,64},{128,96},{160,128},{192,160},{224,192},{256... | collective-permute-start | bytes 122888 | tf_op jit(solution)/shard_map/while/body/eval_jaxpr/ppermute | solution.py:14
  102.6 5.0 %collective-permute-start = (f32[5,2048]{1,0:T(8,128)S(1)}, f32[5,2048]{1,0:T(8,128)S(1)}, u32[]{:S(2)}, u32[]{:S(2)}) collective-permute-start(f32[5,2048]{1,0:T(8,128)S(1)} %add.124), channel_id=1, source_target_pairs={{32,0},{64,32},{96,64},{128,96},{160,128},{192,160},{224,192},{256... | collective-permute-start | bytes 122888 | tf_op jit(solution)/shard_map/while/body/eval_jaxpr/ppermute | solution.py:14
  107.7 5.0 %collective-permute-start = (f32[5,2048]{1,0:T(8,128)S(1)}, f32[5,2048]{1,0:T(8,128)S(1)}, u32[]{:S(2)}, u32[]{:S(2)}) collective-permute-start(f32[5,2048]{1,0:T(8,128)S(1)} %add.124), channel_id=1, source_target_pairs={{32,0},{64,32},{96,64},{128,96},{160,128},{192,160},{224,192},{256... | collective-permute-start | bytes 122888 | tf_op jit(solution)/shard_map/while/body/eval_jaxpr/ppermute | solution.py:14
  112.9 6.4 %collective-permute-start = (f32[5,2048]{1,0:T(8,128)S(1)}, f32[5,2048]{1,0:T(8,128)S(1)}, u32[]{:S(2)}, u32[]{:S(2)}) collective-permute-start(f32[5,2048]{1,0:T(8,128)S(1)} %add.124), channel_id=1, source_target_pairs={{32,0},{64,32},{96,64},{128,96},{160,128},{192,160},{224,192},{256... | collective-permute-start | bytes 122888 | tf_op jit(solution)/shard_map/while/body/eval_jaxpr/ppermute | solution.py:14
  119.4 7.1 %collective-permute-start = (f32[5,2048]{1,0:T(8,128)S(1)}, f32[5,2048]{1,0:T(8,128)S(1)}, u32[]{:S(2)}, u32[]{:S(2)}) collective-permute-start(f32[5,2048]{1,0:T(8,128)S(1)} %add.124), channel_id=1, source_target_pairs={{32,0},{64,32},{96,64},{128,96},{160,128},{192,160},{224,192},{256... | collective-permute-start | bytes 122888 | tf_op jit(solution)/shard_map/while/body/eval_jaxpr/ppermute | solution.py:14
  126.6 7.1 %collective-permute-start = (f32[5,2048]{1,0:T(8,128)S(1)}, f32[5,2048]{1,0:T(8,128)S(1)}, u32[]{:S(2)}, u32[]{:S(2)}) collective-permute-start(f32[5,2048]{1,0:T(8,128)S(1)} %add.124), channel_id=1, source_target_pairs={{32,0},{64,32},{96,64},{128,96},{160,128},{192,160},{224,192},{256... | collective-permute-start | bytes 122888 | tf_op jit(solution)/shard_map/while/body/eval_jaxpr/ppermute | solution.py:14
  133.9 7.1 %collective-permute-start = (f32[5,2048]{1,0:T(8,128)S(1)}, f32[5,2048]{1,0:T(8,128)S(1)}, u32[]{:S(2)}, u32[]{:S(2)}) collective-permute-start(f32[5,2048]{1,0:T(8,128)S(1)} %add.124), channel_id=1, source_target_pairs={{32,0},{64,32},{96,64},{128,96},{160,128},{192,160},{224,192},{256... | collective-permute-start | bytes 122888 | tf_op jit(solution)/shard_map/while/body/eval_jaxpr/ppermute | solution.py:14
  141.1 7.1 %collective-permute-start = (f32[5,2048]{1,0:T(8,128)S(1)}, f32[5,2048]{1,0:T(8,128)S(1)}, u32[]{:S(2)}, u32[]{:S(2)}) collective-permute-start(f32[5,2048]{1,0:T(8,128)S(1)} %add.124), channel_id=1, source_target_pairs={{32,0},{64,32},{96,64},{128,96},{160,128},{192,160},{224,192},{256... | collective-permute-start | bytes 122888 | tf_op jit(solution)/shard_map/while/body/eval_jaxpr/ppermute | solution.py:14
  148.4 8.0 %collective-permute-start = (f32[5,2048]{1,0:T(8,128)S(1)}, f32[5,2048]{1,0:T(8,128)S(1)}, u32[]{:S(2)}, u32[]{:S(2)}) collective-permute-start(f32[5,2048]{1,0:T(8,128)S(1)} %add.124), channel_id=1, source_target_pairs={{32,0},{64,32},{96,64},{128,96},{160,128},{192,160},{224,192},{256... | collective-permute-start | bytes 122888 | tf_op jit(solution)/shard_map/while/body/eval_jaxpr/ppermute | solution.py:14
  156.5 7.2 %collective-permute-start = (f32[5,2048]{1,0:T(8,128)S(1)}, f32[5,2048]{1,0:T(8,128)S(1)}, u32[]{:S(2)}, u32[]{:S(2)}) collective-permute-start(f32[5,2048]{1,0:T(8,128)S(1)} %add.124), channel_id=1, source_target_pairs={{32,0},{64,32},{96,64},{128,96},{160,128},{192,160},{224,192},{256... | collective-permute-start | bytes 122888 | tf_op jit(solution)/shard_map/while/body/eval_jaxpr/ppermute | solution.py:14
  163.8 7.7 %collective-permute-start = (f32[5,2048]{1,0:T(8,128)S(1)}, f32[5,2048]{1,0:T(8,128)S(1)}, u32[]{:S(2)}, u32[]{:S(2)}) collective-permute-start(f32[5,2048]{1,0:T(8,128)S(1)} %add.124), channel_id=1, source_target_pairs={{32,0},{64,32},{96,64},{128,96},{160,128},{192,160},{224,192},{256... | collective-permute-start | bytes 122888 | tf_op jit(solution)/shard_map/while/body/eval_jaxpr/ppermute | solution.py:14
  171.6 6.6 %collective-permute-start = (f32[5,2048]{1,0:T(8,128)S(1)}, f32[5,2048]{1,0:T(8,128)S(1)}, u32[]{:S(2)}, u32[]{:S(2)}) collective-permute-start(f32[5,2048]{1,0:T(8,128)S(1)} %add.124), channel_id=1, source_target_pairs={{32,0},{64,32},{96,64},{128,96},{160,128},{192,160},{224,192},{256... | collective-permute-start | bytes 122888 | tf_op jit(solution)/shard_map/while/body/eval_jaxpr/ppermute | solution.py:14
  178.3 7.1 %collective-permute-start = (f32[5,2048]{1,0:T(8,128)S(1)}, f32[5,2048]{1,0:T(8,128)S(1)}, u32[]{:S(2)}, u32[]{:S(2)}) collective-permute-start(f32[5,2048]{1,0:T(8,128)S(1)} %add.124), channel_id=1, source_target_pairs={{32,0},{64,32},{96,64},{128,96},{160,128},{192,160},{224,192},{256... | collective-permute-start | bytes 122888 | tf_op jit(solution)/shard_map/while/body/eval_jaxpr/ppermute | solution.py:14
  185.6 7.1 %collective-permute-start = (f32[5,2048]{1,0:T(8,128)S(1)}, f32[5,2048]{1,0:T(8,128)S(1)}, u32[]{:S(2)}, u32[]{:S(2)}) collective-permute-start(f32[5,2048]{1,0:T(8,128)S(1)} %add.124), channel_id=1, source_target_pairs={{32,0},{64,32},{96,64},{128,96},{160,128},{192,160},{224,192},{256... | collective-permute-start | bytes 122888 | tf_op jit(solution)/shard_map/while/body/eval_jaxpr/ppermute | solution.py:14
  192.8 7.1 %collective-permute-start = (f32[5,2048]{1,0:T(8,128)S(1)}, f32[5,2048]{1,0:T(8,128)S(1)}, u32[]{:S(2)}, u32[]{:S(2)}) collective-permute-start(f32[5,2048]{1,0:T(8,128)S(1)} %add.124), channel_id=1, source_target_pairs={{32,0},{64,32},{96,64},{128,96},{160,128},{192,160},{224,192},{256... | collective-permute-start | bytes 122888 | tf_op jit(solution)/shard_map/while/body/eval_jaxpr/ppermute | solution.py:14
  245.2 15.9 %copy-start.2 = (f32[256]{0:T(256)S(1)}, f32[256]{0:T(256)}, u32[]{:S(2)}) copy-start(f32[256]{0:T(256)} %param.25) | copy-start | bytes 3076
  245.2 15.9 %copy-start.3 = (s32[256]{0:T(256)S(1)}, s32[256]{0:T(256)}, u32[]{:S(2)}) copy-start(s32[256]{0:T(256)} %param.23) | copy-start | bytes 3076
  245.3 143.2 %copy-start.1 = (f32[3,5,256]{2,0,1:T(4,128)S(1)}, f32[3,5,256]{2,0,1:T(4,128)}, u32[]{:S(2)}) copy-start(f32[3,5,256]{2,0,1:T(4,128)} %param.24) | copy-start | bytes 46084
  391.3 22.6 %all-to-all-start = ((f32[3,32,16]{2,0,1:T(4,128)}), f32[3,32,16]{2,0,1:T(4,128)S(1)}, u32[]{:S(2)}, u32[]{:S(2)}) async-start(f32[3,32,16]{2,0,1:T(4,128)} %copy.49), calls=%async_computation | async-start | bytes 131072 | tf_op jit(solution)/shard_map/all_to_all | solution.py:108
where the time goes:
time: 419 us; the launch traced here: 415 us
  blocking collectives  127 us (30%)
  waiting for transfers between devices  94.4 us (23%)
  other arithmetic  89.6 us (21%)
  local copies, waits for them, and re-layouts  54 us (13%)
  starting transfers between devices  45.6 us (11%)
    psum x1, blocking collectives, on_device(): hinge = lax.psum(hinge_local, ('span', 'plane')) / math.sqrt(all_faces)  127 us
    ppermute x15, waiting for transfers between devices, shifted(): return lax.ppermute(block, axis, route)  81.5 us
    dynamic_update_slice x32, other arithmetic, on_device(): lax.scan(compose_plane, (identity_blk, empty_vec), planes_in, reverse=True)  25.9 us
    reduce_sum x47, other arithmetic, apply_block(): return jnp.sum(matrix * vector[None, :, :], axis=1)  21 us
    ppermute x15, starting transfers between devices, shifted(): return lax.ppermute(block, axis, route)  19.4 us
    all_to_all x1, starting transfers between devices, on_device(): lax.all_to_all(sent[1], 'plane', split_axis=1, concat_axis=1, tiled=True)  16.7 us
    transpose x16, other arithmetic, plane_terms(): upper_t = jnp.swapaxes(upper_block, 0, 1)  15.4 us
    add x16, other arithmetic, sweep_plane(): present_state = apply_block(coupling, above) + source  13.8 us
  transfers between devices with their start and end apart: 17, of which 16 were waited for; matrix products, arithmetic and copies ran while one was open for 34% of the time, Pallas kernels for 0%

commit v1 on v0

v1 whole, which is shorter than its diff:
```python
import math

import jax
import jax.numpy as jnp
from jax import lax
from jax.experimental import pallas as pl
from jax.experimental.pallas import tpu as pltpu
from jax.sharding import PartitionSpec as P

MESH = pl.DeviceIdType.MESH

FIELDS = 5
LOADS = 3
NS = 16
NP = 32
PLANES = 16
CELLS = 2048
LANES = 128
CHUNKS = CELLS // LANES
HALF = CHUNKS // 2
FACES = 256
SHELL = 128
CAP = 16
COMPS = FIELDS * (FIELDS + 1)
MAP_ROWS = 32
ROWS = CHUNKS * PLANES
GROUPS = 4
GROUP_CELLS = CELLS // GROUPS
GROUP_CHUNKS = CHUNKS // GROUPS
HINGE_AT = 0
LOAD_AT = 16
SLOT_AT = 64


def chunk_of(dev):
    x, y = dev // 4, dev % 4
    return HALF * ((x + y) % 2) + 2 * x + y // 2


def device_of(half, j):
    x = j // 2
    return 4 * x + 2 * (j % 2) + (half + x) % 2


def split(value):
    high = value.astype(jnp.bfloat16)
    low = (value - high.astype(jnp.float32)).astype(jnp.bfloat16)
    return high, low


def kernel(
    forcing,
    inv_diag,
    upper,
    cell,
    owner,
    slot,
    count,
    aileron,
    fmap,
    arm,
    adj_out,
    shell_out,
    hinge_out,
    f_v,
    d_v,
    u_v,
    cell_v,
    owner_v,
    slot_v,
    ail_v,
    fmap_v,
    arm_v,
    terms,
    maps,
    maps_in,
    inc_out,
    inc_in,
    adj,
    hot,
    msg,
    msg_in,
    hmsg,
    hmsg_in,
    load_sem,
    small_sem,
    out_sem,
    map_ssem,
    map_rsem,
    inc_ssem,
    inc_rsem,
    face_ssem,
    face_rsem,
    hinge_ssem,
    hinge_rsem,
):
    me = lax.axis_index("span")
    q = lax.axis_index("plane")
    barrier = pltpu.get_barrier_semaphore()

    def load_copies(g):
        cells = pl.ds(g * GROUP_CELLS, GROUP_CELLS)
        return (
            pltpu.make_async_copy(
                inv_diag.at[:, :, :, cells], d_v.at[:, :, :, cells], load_sem.at[g, 0]
            ),
            pltpu.make_async_copy(
                upper.at[:, :, :, cells], u_v.at[:, :, :, cells], load_sem.at[g, 1]
            ),
            pltpu.make_async_copy(
                forcing.at[:, :, cells], f_v.at[:, :, cells], load_sem.at[g, 2]
            ),
        )

    for g in range(GROUPS):
        for copy in load_copies(g):
            copy.start()
    small = [
        pltpu.make_async_copy(src, dst, small_sem.at[n])
        for n, (src, dst) in enumerate(
            (
                (cell, cell_v),
                (owner, owner_v),
                (slot, slot_v),
                (aileron, ail_v),
                (fmap, fmap_v),
                (arm, arm_v),
            )
        )
    ]
    for copy in small:
        copy.start()

    def greet_span(r, carry):
        pl.semaphore_signal(
            barrier, inc=1, device_id=((me + r) % NS, q), device_id_type=MESH
        )
        return carry

    def greet_plane(r, carry):
        pl.semaphore_signal(
            barrier, inc=1, device_id=(me, (q + r) % NP), device_id_type=MESH
        )
        return carry

    lax.fori_loop(1, NS, greet_span, 0)
    lax.fori_loop(1, NP, greet_plane, 0)
    inc_out[...] = jnp.zeros_like(inc_out)

    def chunk_terms(c, carry):
        cells = pl.ds(pl.multiple_of(c * LANES, LANES), LANES)
        rows = pl.ds(pl.multiple_of(c * PLANES, PLANES), PLANES)
        up = [
            [u_v[j, m, :, cells].astype(jnp.float32) for m in range(FIELDS)]
            for j in range(FIELDS)
        ]
        rhs = [f_v[m, :, cells] for m in range(FIELDS)]
        for i in range(FIELDS):
            inv = [d_v[m, i, :, cells].astype(jnp.float32) for m in range(FIELDS)]
            for j in range(FIELDS):
                total = inv[0] * up[j][0]
                for m in range(1, FIELDS):
                    total = total + inv[m] * up[j][m]
                terms[i * FIELDS + j, rows, :] = -total
            total = inv[0] * rhs[0]
            for m in range(1, FIELDS):
                total = total + inv[m] * rhs[m]
            terms[FIELDS * FIELDS + i, rows, :] = total
        return carry

    def term(n, half, k):
        return terms[n, pl.ds(half * HALF * PLANES + k, HALF, stride=PLANES), :]

    def matvec(coupling, vec, start=None):
        out = []
        for i in range(FIELDS):
            total = coupling[i * FIELDS] * vec[0]
            for j in range(1, FIELDS):
                total = total + coupling[i * FIELDS + j] * vec[j]
            out.append(total if start is None else total + start[i])
        return out

    def section_map(half):
        state = tuple(term(n, half, PLANES - 1) for n in range(COMPS))

        def compose(step, state):
            k = PLANES - 2 - step
            coupling = [term(n, half, k) for n in range(FIELDS * FIELDS)]
            source = [term(FIELDS * FIELDS + i, half, k) for i in range(FIELDS)]
            new = [None] * COMPS
            for col in range(FIELDS):
                column = matvec(coupling, [state[j * FIELDS + col] for j in range(FIELDS)])
                for i in range(FIELDS):
                    new[i * FIELDS + col] = column[i]
            new[FIELDS * FIELDS :] = matvec(coupling, state[FIELDS * FIELDS :], source)
            return tuple(new)

        state = lax.fori_loop(0, PLANES - 1, compose, state)
        for n in range(COMPS):
            maps[pl.ds(half * HALF * MAP_ROWS + n, HALF, stride=MAP_ROWS), :] = state[n]

    def map_rows(c):
        return pl.ds(pl.multiple_of(c * MAP_ROWS, MAP_ROWS), MAP_ROWS)

    def map_copy(c, dest, source):
        return pltpu.make_async_remote_copy(
            src_ref=maps.at[map_rows(c), :],
            dst_ref=maps_in.at[map_rows(source), :],
            send_sem=map_ssem.at[dest],
            recv_sem=map_rsem.at[source],
            device_id=(dest, q),
            device_id_type=MESH,
        )

    for n in range(COMPS, MAP_ROWS):
        maps[pl.ds(n, CHUNKS, stride=MAP_ROWS), :] = jnp.zeros((CHUNKS, LANES), jnp.float32)

    my_chunk = chunk_of(me)
    my_j = my_chunk % HALF
    for half in range(2):
        for g in range(half * GROUPS // 2, (half + 1) * GROUPS // 2):
            for copy in load_copies(g):
                copy.wait()
            lax.fori_loop(g * GROUP_CHUNKS, (g + 1) * GROUP_CHUNKS, chunk_terms, 0)
        section_map(half)
        if half == 0:
            pl.semaphore_wait(barrier, NS - 1 + NP - 1)

        def send_map(t, carry):
            j = (my_j + t) % HALF
            dest = device_of(half, j)

            @pl.when(dest != me)
            def _():
                map_copy(half * HALF + j, dest, me).start()

            return carry

        lax.fori_loop(0, HALF, send_map, 0)

    for copy in small:
        copy.wait()
    face_cell = cell_v[...].reshape(1, FACES)
    face_plane = face_cell // CELLS
    face_at = face_cell % CELLS
    for c in range(CHUNKS):
        at = lax.broadcasted_iota(jnp.int32, (LANES, FACES), 0) + c * LANES
        hot[pl.ds(c * LANES, LANES), :] = jnp.where(at == face_at, 1.0, 0.0).astype(jnp.bfloat16)
    plane_hit = lax.broadcasted_iota(jnp.int32, (PLANES, FACES), 0) == face_plane
    face_id = lax.broadcasted_iota(jnp.int32, (1, FACES), 1)
    live = jnp.where(face_id < count[0], 1.0, 0.0)
    owner_hot = jnp.where(
        lax.broadcasted_iota(jnp.int32, (NP, FACES), 0) == owner_v[...], 1.0, 0.0
    )
    owner_hot16 = owner_hot.astype(jnp.bfloat16)
    earlier = jnp.where(
        lax.broadcasted_iota(jnp.int32, (FACES, FACES), 0)
        < lax.broadcasted_iota(jnp.int32, (FACES, FACES), 1),
        1.0,
        0.0,
    ).astype(jnp.bfloat16)
    before = jnp.dot(owner_hot16, earlier, preferred_element_type=jnp.float32)
    rank = jnp.sum(owner_hot * before, axis=0, keepdims=True).astype(jnp.int32)
    rank_hot = jnp.where(lax.broadcasted_iota(jnp.int32, (CAP, FACES), 0) == rank, 1.0, 0.0)
    slot_value = (slot_v[...].reshape(1, FACES) + 1).astype(jnp.float32) * live
    slot_rows = rank_hot * slot_value
    weight = ail_v[...].reshape(1, FACES).astype(jnp.float32) * live * arm_v[...].reshape(1, FACES)

    maps_in[map_rows(me), :] = maps[map_rows(my_chunk), :]
    vec = [jnp.zeros((1, LANES), jnp.float32) for _ in range(FIELDS)]
    for section in range(NS - 1, 0, -1):

        @pl.when(me != section)
        def _():
            map_copy(0, section, section).wait_recv()

        def entry(n):
            return maps_in[pl.ds(section * MAP_ROWS + n, 1), :]

        matrix = [entry(n) for n in range(FIELDS * FIELDS)]
        vec = matvec(matrix, vec, [entry(FIELDS * FIELDS + i) for i in range(FIELDS)])
        for i in range(FIELDS):
            inc_out[pl.ds((section - 1) * 8 + i, 1), :] = vec[i]

    @pl.when(me != 0)
    def _():
        map_copy(0, 0, 0).wait_recv()

    def inc_copy(dest, c, source):
        return pltpu.make_async_remote_copy(
            src_ref=inc_out.at[pl.ds(pl.multiple_of(dest * 8, 8), 8), :],
            dst_ref=inc_in.at[pl.ds(pl.multiple_of(c * 8, 8), 8), :],
            send_sem=inc_ssem.at[dest],
            recv_sem=inc_rsem.at[source],
            device_id=(dest, q),
            device_id_type=MESH,
        )

    def send_inc(r, carry):
        inc_copy((me + r) % NS, my_chunk, me).start()
        return carry

    lax.fori_loop(1, NS, send_inc, 0)
    inc_in[pl.ds(pl.multiple_of(my_chunk * 8, 8), 8), :] = inc_out[
        pl.ds(pl.multiple_of(me * 8, 8), 8), :
    ]

    gathered = jnp.zeros((2 * FIELDS * PLANES, FACES), jnp.float32)
    outputs = []
    for half in range(2):
        for j in range(HALF):
            dev = device_of(half, j)

            @pl.when(me != dev)
            def _():
                inc_copy(dev, half * HALF + j, dev).wait_recv()

        state = tuple(
            inc_in[pl.ds(half * HALF * 8 + i, HALF, stride=8), :] for i in range(FIELDS)
        )

        def sweep(step, state):
            k = PLANES - 1 - step
            coupling = [term(n, half, k) for n in range(FIELDS * FIELDS)]
            source = [term(FIELDS * FIELDS + i, half, k) for i in range(FIELDS)]
            state = matvec(coupling, state, source)
            for i in range(FIELDS):
                adj[i, pl.ds(half * HALF * PLANES + k, HALF, stride=PLANES), :] = state[i]
            return tuple(state)

        lax.fori_loop(0, PLANES, sweep, state)
        for c in range(half * HALF, (half + 1) * HALF):
            copy = pltpu.make_async_copy(
                adj.at[:, pl.ds(c * PLANES, PLANES), :],
                adj_out.at[:, :, pl.ds(c * LANES, LANES)],
                out_sem.at[c],
            )
            copy.start()
            outputs.append(copy)
        for c in range(half * HALF, (half + 1) * HALF, 2):
            pair = jnp.concatenate(
                [
                    adj[:, pl.ds(e * PLANES, PLANES), :].reshape(FIELDS * PLANES, LANES)
                    for e in (c, c + 1)
                ],
                axis=1,
            )
            gathered = gathered + jnp.dot(
                jnp.concatenate(split(pair), axis=0),
                hot[pl.ds(c * LANES, 2 * LANES), :],
                preferred_element_type=jnp.float32,
            )

    both = gathered[: FIELDS * PLANES] + gathered[FIELDS * PLANES :]
    rows = [
        jnp.sum(
            jnp.where(plane_hit, both[i * PLANES : (i + 1) * PLANES], 0.0), axis=0, keepdims=True
        )
        for i in range(FIELDS)
    ]
    load_rows = []
    for a in range(LOADS):
        total = fmap_v[0, pl.ds(a, 1), :] * rows[0]
        for i in range(1, FIELDS):
            total = total + fmap_v[i, pl.ds(a, 1), :] * rows[i]
        load_rows.append(rank_hot * (total * live))
    hinge_rows = jnp.concatenate(
        [rows[i] * weight for i in range(FIELDS)]
        + [jnp.zeros((LANES - FIELDS, FACES), jnp.float32)],
        axis=0,
    )
    face_rows = jnp.concatenate(
        [jnp.zeros((LOAD_AT, FACES), jnp.float32)]
        + load_rows
        + [slot_rows, jnp.zeros((LANES - SLOT_AT - CAP, FACES), jnp.float32)],
        axis=0,
    )

    def by_face(left, right):
        return lax.dot_general(
            left, right, (((1,), (1,)), ((), ())), preferred_element_type=jnp.float32
        )

    every = jnp.ones((NP, FACES), jnp.bfloat16)
    packed = jnp.zeros((NP, LANES), jnp.float32)
    for piece in split(face_rows):
        packed = packed + by_face(owner_hot16, piece)
    for piece in split(hinge_rows):
        packed = packed + by_face(every, piece)
    msg[:, 0, :] = packed

    def face_copy(dest, source):
        return pltpu.make_async_remote_copy(
            src_ref=msg.at[dest],
            dst_ref=msg_in.at[source],
            send_sem=face_ssem.at[dest],
            recv_sem=face_rsem.at[source],
            device_id=(me, dest),
            device_id_type=MESH,
        )

    def send_face(r, carry):
        face_copy((q + r) % NP, q).start()
        return carry

    lax.fori_loop(1, NP, send_face, 0)
    msg_in[q] = msg[q]

    def wait_face(r, carry):
        peer = (q + r) % NP
        face_copy(peer, peer).wait_recv()
        return carry

    lax.fori_loop(1, NP, wait_face, 0)
    arrived = msg_in[:, 0, :]

    hmsg[0] = jnp.sum(arrived, axis=0, keepdims=True)

    def hinge_copy(dest, source):
        return pltpu.make_async_remote_copy(
            src_ref=hmsg.at[0],
            dst_ref=hmsg_in.at[source],
            send_sem=hinge_ssem.at[dest],
            recv_sem=hinge_rsem.at[source],
            device_id=(dest, q),
            device_id_type=MESH,
        )

    def send_hinge(r, carry):
        hinge_copy((me + r) % NS, me).start()
        return carry

    lax.fori_loop(1, NS, send_hinge, 0)
    hmsg_in[me] = hmsg[0]

    lane = lax.broadcasted_iota(jnp.int32, (NP, LANES), 1) + 1
    loads = [jnp.zeros((NP, SHELL), jnp.float32) for _ in range(LOADS)]
    for pos in range(CAP):
        at = SLOT_AT + pos
        hit = arrived[:, at : at + 1].astype(jnp.int32) == lane
        for a in range(LOADS):
            at = LOAD_AT + a * CAP + pos
            loads[a] = loads[a] + jnp.where(hit, arrived[:, at : at + 1], 0.0)
    for a in range(LOADS):
        shell_out[pl.ds(a, 1), :] = jnp.sum(loads[a], axis=0, keepdims=True)

    for copy in outputs:
        copy.wait()

    def sent(r, carry):
        peer = (me + r) % NS
        map_copy(0, peer, peer).wait_send()
        inc_copy(peer, 0, peer).wait_send()
        return carry

    lax.fori_loop(1, NS, sent, 0)

    def sent_face(r, carry):
        peer = (q + r) % NP
        face_copy(peer, peer).wait_send()
        return carry

    lax.fori_loop(1, NP, sent_face, 0)

    def wait_hinge(r, carry):
        peer = (me + r) % NS
        hinge_copy(peer, peer).wait_send()
        hinge_copy(peer, peer).wait_recv()
        return carry

    lax.fori_loop(1, NS, wait_hinge, 0)
    total = jnp.sum(hmsg_in[:, 0, :], axis=0) * (1.0 / math.sqrt(NS * NP * FACES))
    hinge_out[...] = total[:FIELDS]


def on_device(
    forcing,
    inv_diag,
    upper_jac,
    face_cell,
    face_owner,
    face_slot,
    face_count,
    aileron,
    face_map,
    hinge_arm,
):
    anywhere = pl.BlockSpec(memory_space=pl.ANY)
    vmem = pl.BlockSpec(memory_space=pltpu.VMEM)
    f32, bf16, i32 = jnp.float32, jnp.bfloat16, jnp.int32
    dma = pltpu.SemaphoreType.DMA
    return pl.pallas_call(
        kernel,
        out_shape=(
            jax.ShapeDtypeStruct((FIELDS, PLANES, CELLS), f32),
            jax.ShapeDtypeStruct((LOADS, SHELL), f32),
            jax.ShapeDtypeStruct((FIELDS,), f32),
        ),
        in_specs=[anywhere] * 6
        + [pl.BlockSpec(memory_space=pltpu.SMEM)]
        + [anywhere] * 3,
        out_specs=(anywhere, vmem, vmem),
        scratch_shapes=[
            pltpu.VMEM((FIELDS, PLANES, CELLS), f32),
            pltpu.VMEM((FIELDS, FIELDS, PLANES, CELLS), bf16),
            pltpu.VMEM((FIELDS, FIELDS, PLANES, CELLS), bf16),
            pltpu.VMEM((FACES,), i32),
            pltpu.VMEM((1, FACES), i32),
            pltpu.VMEM((FACES,), i32),
            pltpu.VMEM((FACES,), i32),
            pltpu.VMEM((FIELDS, LOADS, FACES), f32),
            pltpu.VMEM((FACES,), f32),
            pltpu.VMEM((COMPS, ROWS, LANES), f32),
            pltpu.VMEM((CHUNKS * MAP_ROWS, LANES), f32),
            pltpu.VMEM((NS * MAP_ROWS, LANES), f32),
            pltpu.VMEM((NS * 8, LANES), f32),
            pltpu.VMEM((CHUNKS * 8, LANES), f32),
            pltpu.VMEM((FIELDS, ROWS, LANES), f32),
            pltpu.VMEM((CELLS, FACES), bf16),
            pltpu.VMEM((NP, 1, LANES), f32),
            pltpu.VMEM((NP, 1, LANES), f32),
            pltpu.VMEM((1, 1, LANES), f32),
            pltpu.VMEM((NS, 1, LANES), f32),
            dma((GROUPS, 3)),
            dma((6,)),
            dma((CHUNKS,)),
            dma((NS,)),
            dma((NS,)),
            dma((NS,)),
            dma((NS,)),
            dma((NP,)),
            dma((NP,)),
            dma((NS,)),
            dma((NS,)),
        ],
        compiler_params=pltpu.CompilerParams(
            collective_id=0, has_side_effects=True, vmem_limit_bytes=48 * 1024 * 1024
        ),
        cost_estimate=pl.CostEstimate(
            flops=22_000_000, bytes_accessed=4_700_000, transcendentals=0
        ),
        name="sweep",
    )(
        forcing,
        inv_diag,
        upper_jac,
        face_cell,
        face_owner.T,
        face_slot,
        face_count,
        aileron,
        jnp.swapaxes(face_map, 0, 1),
        hinge_arm,
    )


def solution(mesh):
    in_specs = (
        P(None, "span", "plane"),
        P(None, None, "span", "plane"),
        P(None, None, "span", "plane"),
        P(("span", "plane")),
        P(("span", "plane"), None),
        P(("span", "plane")),
        P(("span", "plane")),
        P(("span", "plane")),
        P(None, None, ("span", "plane")),
        P(("span", "plane")),
    )
    out_specs = (P(None, "span", "plane"), P(None, ("span", "plane")), P())
    return jax.shard_map(
        on_device, mesh=mesh, in_specs=in_specs, out_specs=out_specs, check_vma=False
    )
```

time: 419 us -> 56 us (0.13)
  blocking collectives: 127 us -> 0 us
  waiting for transfers between devices: 94.4 us -> 0 us
  other arithmetic: 89.6 us -> 0 us
  starting transfers between devices: 45.6 us -> 0 us
  Pallas kernels: 0 us -> 44.3 us
  local copies, waits for them, and re-layouts: 54 us -> 9.99 us
    psum x1 -> x0, blocking collectives: 127 us -> none  [on_device(): hinge = lax.psum(hinge_local, ('span', 'plane')) / math.sqrt(all_faces)]
    ppermute x15 -> x0, waiting for transfers between devices: 81.5 us -> none  [shifted(): return lax.ppermute(block, axis, route)]
    pallas_call x0 -> x1, Pallas kernels: none -> 44.3 us  [on_device(): pl.pallas_call(kernel, out_shape=(jax.ShapeDtypeStruct((FIELDS, PLANES, C...]
    reduce_sum x99 -> x0, other arithmetic: 29.3 us -> none  [the longest x47 21 us: apply_block(): return jnp.sum(matrix * vector[None, :, :], axis=1)]
    all_to_all x2 -> x0, starting transfers between devices: 26.2 us -> none  [the longest x1 16.7 us: on_device(): lax.all_to_all(sent[1], 'plane', split_axis=1, concat_axis=1, tiled=True)]
    dynamic_update_slice x32 -> x0, other arithmetic: 25.9 us -> none  [on_device(): lax.scan(compose_plane, (identity_blk, empty_vec), planes_in, reverse=True)]
    ppermute x15 -> x0, starting transfers between devices: 19.4 us -> none  [shifted(): return lax.ppermute(block, axis, route)]
    add x49 -> x0, other arithmetic: 15.5 us -> none  [the longest x16 13.8 us: sweep_plane(): present_state = apply_block(coupling, above) + source]
  transfers between devices with their start and end apart: 17 -> 0, of which waited for: 16 -> 0; matrix products, arithmetic and copies ran while one was open for 34% -> 0% of each run, Pallas kernels for 0% -> 0%
where the time goes in v1:
time: 56 us; the launch traced here: 55.6 us
  Pallas kernels  44.3 us (79%)
  local copies, waits for them, and re-layouts  9.99 us (18%)
  between operations  1.31 us (2%)
    pallas_call x1, Pallas kernels, on_device(): pl.pallas_call(kernel, out_shape=(jax.ShapeDtypeStruct((FIELDS, PLANES, C...  44.3 us
    unnamed x21, local copies, waits for them, and re-layouts  9.99 us

profile of v1, /device:TPU:1, one launch (start us, length us, event | category | flops | bytes accessed | tf_op | source)
XLA Modules:
  0.0 55.6 jit_solution(11470624807554936417)
XLA Ops:
  1.3 0.0 copy-start
  1.3 1.4 %copy-done = bf16[5,5,16,2048]{3,2,1,0:T(8,128)(2,1)S(1)} copy-done((bf16[5,5,16,2048]{3,2,1,0:T(8,128)(2,1)S(1)}, bf16[5,5,16,2048]{3,2,1,0:T(8,128)(2,1)}, u32[]{:S(2)}) %copy-start) | copy-done | bytes 1638424
  2.7 0.0 copy-start.1
  2.7 1.4 %copy-done.1 = bf16[5,5,16,2048]{3,2,1,0:T(8,128)(2,1)S(1)} copy-done((bf16[5,5,16,2048]{3,2,1,0:T(8,128)(2,1)S(1)}, bf16[5,5,16,2048]{3,2,1,0:T(8,128)(2,1)}, u32[]{:S(2)}) %copy-start.1) | copy-done | bytes 1638424
  4.1 0.0 copy-start.2
  4.1 1.1 %copy-done.2 = f32[5,16,2048]{2,1,0:T(8,128)S(1)} copy-done((f32[5,16,2048]{2,1,0:T(8,128)S(1)}, f32[5,16,2048]{2,1,0:T(8,128)}, u32[]{:S(2)}) %copy-start.2) | copy-done | bytes 655384
  5.2 0.0 copy-start.3
  5.2 0.7 %copy-done.3 = f32[3,5,256]{2,0,1:T(4,128)S(1)} copy-done((f32[3,5,256]{2,0,1:T(4,128)S(1)}, f32[3,5,256]{2,0,1:T(4,128)}, u32[]{:S(2)}) %copy-start.3) | copy-done | bytes 15384
  6.0 0.0 copy-start.4
  6.0 0.7 %copy-done.4 = s32[256]{0:T(256)S(1)} copy-done((s32[256]{0:T(256)S(1)}, s32[256]{0:T(256)}, u32[]{:S(2)}) %copy-start.4) | copy-done | bytes 1048
  6.6 0.0 copy-start.5
  6.6 0.7 %copy-done.5 = s32[256,1]{0,1:T(1,128)S(1)} copy-done((s32[256,1]{0,1:T(1,128)S(1)}, s32[256,1]{0,1:T(1,128)}, u32[]{:S(2)}) %copy-start.5) | copy-done | bytes 1048
  7.3 0.0 copy-start.6
  7.3 0.7 %copy-done.6 = s32[256]{0:T(256)S(1)} copy-done((s32[256]{0:T(256)S(1)}, s32[256]{0:T(256)}, u32[]{:S(2)}) %copy-start.6) | copy-done | bytes 1048
  8.0 0.0 copy-start.7
  8.0 0.7 %copy-done.7 = s32[256]{0:T(256)S(1)} copy-done((s32[256]{0:T(256)S(1)}, s32[256]{0:T(256)}, u32[]{:S(2)}) %copy-start.7) | copy-done | bytes 1048
  8.7 0.0 copy-start.8
  8.7 0.7 %copy-done.8 = f32[256]{0:T(256)S(1)} copy-done((f32[256]{0:T(256)S(1)}, f32[256]{0:T(256)}, u32[]{:S(2)}) %copy-start.8) | copy-done | bytes 1048
  9.4 44.3 %sweep.1 = (f32[5,16,2048]{2,1,0:T(8,128)S(1)}, f32[3,128]{1,0:T(4,128)S(1)}, f32[5]{0:T(128)S(1)}) custom-call(f32[5,16,2048]{2,1,0:T(8,128)S(1)} %copy-done.2, bf16[5,5,16,2048]{3,2,1,0:T(8,128)(2,1)S(1)} %copy-done, bf16[5,5,16,2048]{3,2,1,0:T(8,128)(2,1)S(1)} %copy-done.1, s32[256]{0:T(256)S(1)} %copy-done.4, s32[1,256]{1,0:T(1,128)S(1)} %bitcast.3, ...), custom_call_target="tpu_custom_call" | custom-call | flops 22000000 | bytes 4700000 | tf_op jit(solution)/shard_map/sweep/pallas_call | solution.py:492
  53.7 0.8 %copy.17 = f32[5,16,2048]{2,1,0:T(8,128)} copy(f32[5,16,2048]{2,1,0:T(8,128)S(1)} %get-tuple-element.6) | data formatting | bytes 1310720
  54.5 0.6 %copy.18 = f32[3,128]{1,0:T(4,128)} copy(f32[3,128]{1,0:T(4,128)S(1)} %get-tuple-element.7) | data formatting | bytes 3072
  55.1 0.5 copy.19
Async XLA Ops:
  1.3 1.4 %copy-start = (bf16[5,5,16,2048]{3,2,1,0:T(8,128)(2,1)S(1)}, bf16[5,5,16,2048]{3,2,1,0:T(8,128)(2,1)}, u32[]{:S(2)}) copy-start(bf16[5,5,16,2048]{3,2,1,0:T(8,128)(2,1)} %inv_diag.1) | copy-start | bytes 4915204
  2.7 1.4 %copy-start.1 = (bf16[5,5,16,2048]{3,2,1,0:T(8,128)(2,1)S(1)}, bf16[5,5,16,2048]{3,2,1,0:T(8,128)(2,1)}, u32[]{:S(2)}) copy-start(bf16[5,5,16,2048]{3,2,1,0:T(8,128)(2,1)} %upper.1) | copy-start | bytes 4915204
  4.1 1.1 %copy-start.2 = (f32[5,16,2048]{2,1,0:T(8,128)S(1)}, f32[5,16,2048]{2,1,0:T(8,128)}, u32[]{:S(2)}) copy-start(f32[5,16,2048]{2,1,0:T(8,128)} %forcing.1) | copy-start | bytes 1966084
  5.2 0.7 %copy-start.3 = (f32[3,5,256]{2,0,1:T(4,128)S(1)}, f32[3,5,256]{2,0,1:T(4,128)}, u32[]{:S(2)}) copy-start(f32[3,5,256]{2,0,1:T(4,128)} %param.18) | copy-start | bytes 46084
  6.0 0.7 %copy-start.4 = (s32[256]{0:T(256)S(1)}, s32[256]{0:T(256)}, u32[]{:S(2)}) copy-start(s32[256]{0:T(256)} %cell.1) | copy-start | bytes 3076
  6.6 0.7 %copy-start.5 = (s32[256,1]{0,1:T(1,128)S(1)}, s32[256,1]{0,1:T(1,128)}, u32[]{:S(2)}) copy-start(s32[256,1]{0,1:T(1,128)} %param.14) | copy-start | bytes 3076
  7.3 0.7 %copy-start.6 = (s32[256]{0:T(256)S(1)}, s32[256]{0:T(256)}, u32[]{:S(2)}) copy-start(s32[256]{0:T(256)} %slot.1) | copy-start | bytes 3076
  8.0 0.7 %copy-start.7 = (s32[256]{0:T(256)S(1)}, s32[256]{0:T(256)}, u32[]{:S(2)}) copy-start(s32[256]{0:T(256)} %aileron.1) | copy-start | bytes 3076
  8.7 0.7 %copy-start.8 = (f32[256]{0:T(256)S(1)}, f32[256]{0:T(256)}, u32[]{:S(2)}) copy-start(f32[256]{0:T(256)} %arm.1) | copy-start | bytes 3076

commit v2 on v1

--- a/solution.py
+++ b/solution.py
@@ -23,7 +23,9 @@
 CAP = 16
 COMPS = FIELDS * (FIELDS + 1)
 MAP_ROWS = 32
-ROWS = CHUNKS * PLANES
+MAP_PITCH = 40
+TERM_PITCH = 17
+ADJ_PITCH = 24
 GROUPS = 4
 GROUP_CELLS = CELLS // GROUPS
 GROUP_CHUNKS = CHUNKS // GROUPS
@@ -68,6 +70,7 @@
     cell_v,
     owner_v,
     slot_v,
+    count_s,
     ail_v,
     fmap_v,
     arm_v,
@@ -80,6 +83,7 @@
     hot,
     msg,
     msg_in,
+    rows_in,
     hmsg,
     hmsg_in,
     load_sem,
@@ -122,6 +126,7 @@
                 (cell, cell_v),
                 (owner, owner_v),
                 (slot, slot_v),
+                (count, count_s),
                 (aileron, ail_v),
                 (fmap, fmap_v),
                 (arm, arm_v),
@@ -149,7 +154,7 @@
 
     def chunk_terms(c, carry):
         cells = pl.ds(pl.multiple_of(c * LANES, LANES), LANES)
-        rows = pl.ds(pl.multiple_of(c * PLANES, PLANES), PLANES)
+        rows = pl.ds(c * TERM_PITCH, PLANES)
         up = [
             [u_v[j, m, :, cells].astype(jnp.float32) for m in range(FIELDS)]
             for j in range(FIELDS)
@@ -169,7 +174,7 @@
         return carry
 
     def term(n, half, k):
-        return terms[n, pl.ds(half * HALF * PLANES + k, HALF, stride=PLANES), :]
+        return terms[n, pl.ds(half * HALF * TERM_PITCH + k, HALF, stride=TERM_PITCH), :]
 
     def matvec(coupling, vec, start=None):
         out = []
@@ -197,14 +202,17 @@
 
         state = lax.fori_loop(0, PLANES - 1, compose, state)
         for n in range(COMPS):
-            maps[pl.ds(half * HALF * MAP_ROWS + n, HALF, stride=MAP_ROWS), :] = state[n]
+            maps[pl.ds(half * HALF * MAP_PITCH + n, HALF, stride=MAP_PITCH), :] = state[n]
+
+    def out_rows(c):
+        return pl.ds(pl.multiple_of(c * MAP_PITCH, 8), MAP_ROWS)
 
     def map_rows(c):
         return pl.ds(pl.multiple_of(c * MAP_ROWS, MAP_ROWS), MAP_ROWS)
 
     def map_copy(c, dest, source):
         return pltpu.make_async_remote_copy(
-            src_ref=maps.at[map_rows(c), :],
+            src_ref=maps.at[out_rows(c), :],
             dst_ref=maps_in.at[map_rows(source), :],
             send_sem=map_ssem.at[dest],
             recv_sem=map_rsem.at[source],
@@ -213,7 +221,7 @@
         )
 
     for n in range(COMPS, MAP_ROWS):
-        maps[pl.ds(n, CHUNKS, stride=MAP_ROWS), :] = jnp.zeros((CHUNKS, LANES), jnp.float32)
+        maps[pl.ds(n, CHUNKS, stride=MAP_PITCH), :] = jnp.zeros((CHUNKS, LANES), jnp.float32)
 
     my_chunk = chunk_of(me)
     my_j = my_chunk % HALF
@@ -248,7 +256,7 @@
         hot[pl.ds(c * LANES, LANES), :] = jnp.where(at == face_at, 1.0, 0.0).astype(jnp.bfloat16)
     plane_hit = lax.broadcasted_iota(jnp.int32, (PLANES, FACES), 0) == face_plane
     face_id = lax.broadcasted_iota(jnp.int32, (1, FACES), 1)
-    live = jnp.where(face_id < count[0], 1.0, 0.0)
+    live = jnp.where(face_id < count_s[0], 1.0, 0.0)
     owner_hot = jnp.where(
         lax.broadcasted_iota(jnp.int32, (NP, FACES), 0) == owner_v[...], 1.0, 0.0
     )
@@ -266,7 +274,7 @@
     slot_rows = rank_hot * slot_value
     weight = ail_v[...].reshape(1, FACES).astype(jnp.float32) * live * arm_v[...].reshape(1, FACES)
 
-    maps_in[map_rows(me), :] = maps[map_rows(my_chunk), :]
+    maps_in[map_rows(me), :] = maps[out_rows(my_chunk), :]
     vec = [jnp.zeros((1, LANES), jnp.float32) for _ in range(FIELDS)]
     for section in range(NS - 1, 0, -1):
 
@@ -305,8 +313,6 @@
         pl.ds(pl.multiple_of(me * 8, 8), 8), :
     ]
 
-    gathered = jnp.zeros((2 * FIELDS * PLANES, FACES), jnp.float32)
-    outputs = []
     for half in range(2):
         for j in range(HALF):
             dev = device_of(half, j)
@@ -315,41 +321,47 @@
             def _():
                 inc_copy(dev, half * HALF + j, dev).wait_recv()
 
-        state = tuple(
-            inc_in[pl.ds(half * HALF * 8 + i, HALF, stride=8), :] for i in range(FIELDS)
-        )
-
-        def sweep(step, state):
-            k = PLANES - 1 - step
+    start = tuple(
+        tuple(inc_in[pl.ds(half * HALF * 8 + i, HALF, stride=8), :] for i in range(FIELDS))
+        for half in range(2)
+    )
+
+    def sweep(step, states):
+        k = PLANES - 1 - step
+        new = []
+        for half in range(2):
             coupling = [term(n, half, k) for n in range(FIELDS * FIELDS)]
             source = [term(FIELDS * FIELDS + i, half, k) for i in range(FIELDS)]
-            state = matvec(coupling, state, source)
+            state = matvec(coupling, states[half], source)
             for i in range(FIELDS):
-                adj[i, pl.ds(half * HALF * PLANES + k, HALF, stride=PLANES), :] = state[i]
-            return tuple(state)
-
-        lax.fori_loop(0, PLANES, sweep, state)
-        for c in range(half * HALF, (half + 1) * HALF):
-            copy = pltpu.make_async_copy(
-                adj.at[:, pl.ds(c * PLANES, PLANES), :],
-                adj_out.at[:, :, pl.ds(c * LANES, LANES)],
-                out_sem.at[c],
-            )
-            copy.start()
-            outputs.append(copy)
-        for c in range(half * HALF, (half + 1) * HALF, 2):
-            pair = jnp.concatenate(
-                [
-                    adj[:, pl.ds(e * PLANES, PLANES), :].reshape(FIELDS * PLANES, LANES)
-                    for e in (c, c + 1)
-                ],
-                axis=1,
-            )
-            gathered = gathered + jnp.dot(
-                jnp.concatenate(split(pair), axis=0),
-                hot[pl.ds(c * LANES, 2 * LANES), :],
-                preferred_element_type=jnp.float32,
-            )
+                adj[i, pl.ds(half * HALF * ADJ_PITCH + k, HALF, stride=ADJ_PITCH), :] = state[i]
+            new.append(tuple(state))
+        return tuple(new)
+
+    lax.fori_loop(0, PLANES, sweep, start)
+    outputs = []
+    for c in range(CHUNKS):
+        copy = pltpu.make_async_copy(
+            adj.at[:, pl.ds(c * ADJ_PITCH, PLANES), :],
+            adj_out.at[:, :, pl.ds(c * LANES, LANES)],
+            out_sem.at[c],
+        )
+        copy.start()
+        outputs.append(copy)
+    gathered = jnp.zeros((2 * FIELDS * PLANES, FACES), jnp.float32)
+    for c in range(0, CHUNKS, 2):
+        pair = jnp.concatenate(
+            [
+                adj[:, pl.ds(e * ADJ_PITCH, PLANES), :].reshape(FIELDS * PLANES, LANES)
+                for e in (c, c + 1)
+            ],
+            axis=1,
+        )
+        gathered = gathered + jnp.dot(
+            jnp.concatenate(split(pair), axis=0),
+            hot[pl.ds(c * LANES, 2 * LANES), :],
+            preferred_element_type=jnp.float32,
+        )
 
     both = gathered[: FIELDS * PLANES] + gathered[FIELDS * PLANES :]
     rows = [
@@ -412,7 +424,9 @@
         return carry
 
     lax.fori_loop(1, NP, wait_face, 0)
-    arrived = msg_in[:, 0, :]
+    for peer in range(NP):
+        rows_in[pl.ds(peer, 1), :] = msg_in[peer]
+    arrived = rows_in[...]
 
     hmsg[0] = jnp.sum(arrived, axis=0, keepdims=True)
 
@@ -485,7 +499,7 @@
     face_map,
     hinge_arm,
 ):
-    anywhere = pl.BlockSpec(memory_space=pl.ANY)
+    anywhere = pl.BlockSpec(memory_space=pltpu.HBM)
     vmem = pl.BlockSpec(memory_space=pltpu.VMEM)
     f32, bf16, i32 = jnp.float32, jnp.bfloat16, jnp.int32
     dma = pltpu.SemaphoreType.DMA
@@ -496,9 +510,7 @@
             jax.ShapeDtypeStruct((LOADS, SHELL), f32),
             jax.ShapeDtypeStruct((FIELDS,), f32),
         ),
-        in_specs=[anywhere] * 6
-        + [pl.BlockSpec(memory_space=pltpu.SMEM)]
-        + [anywhere] * 3,
+        in_specs=[anywhere] * 10,
         out_specs=(anywhere, vmem, vmem),
         scratch_shapes=[
             pltpu.VMEM((FIELDS, PLANES, CELLS), f32),
@@ -507,22 +519,24 @@
             pltpu.VMEM((FACES,), i32),
             pltpu.VMEM((1, FACES), i32),
             pltpu.VMEM((FACES,), i32),
+            pltpu.SMEM((1,), i32),
             pltpu.VMEM((FACES,), i32),
             pltpu.VMEM((FIELDS, LOADS, FACES), f32),
             pltpu.VMEM((FACES,), f32),
-            pltpu.VMEM((COMPS, ROWS, LANES), f32),
-            pltpu.VMEM((CHUNKS * MAP_ROWS, LANES), f32),
+            pltpu.VMEM((COMPS, CHUNKS * TERM_PITCH, LANES), f32),
+            pltpu.VMEM((CHUNKS * MAP_PITCH, LANES), f32),
             pltpu.VMEM((NS * MAP_ROWS, LANES), f32),
             pltpu.VMEM((NS * 8, LANES), f32),
             pltpu.VMEM((CHUNKS * 8, LANES), f32),
-            pltpu.VMEM((FIELDS, ROWS, LANES), f32),
+            pltpu.VMEM((FIELDS, CHUNKS * ADJ_PITCH, LANES), f32),
             pltpu.VMEM((CELLS, FACES), bf16),
             pltpu.VMEM((NP, 1, LANES), f32),
             pltpu.VMEM((NP, 1, LANES), f32),
+            pltpu.VMEM((NP, LANES), f32),
             pltpu.VMEM((1, 1, LANES), f32),
             pltpu.VMEM((NS, 1, LANES), f32),
             dma((GROUPS, 3)),
-            dma((6,)),
+            dma((7,)),
             dma((CHUNKS,)),
             dma((NS,)),
             dma((NS,)),
@@ -534,7 +548,7 @@
             dma((NS,)),
         ],
         compiler_params=pltpu.CompilerParams(
-            collective_id=0, has_side_effects=True, vmem_limit_bytes=48 * 1024 * 1024
+            collective_id=0, has_side_effects=True, vmem_limit_bytes=63 * 1024 * 1024
         ),
         cost_estimate=pl.CostEstimate(
             flops=22_000_000, bytes_accessed=4_700_000, transcendentals=0

time: 56 us -> 48.9 us (0.87)
  local copies, waits for them, and re-layouts: 9.99 us -> 4.36 us
  Pallas kernels: 44.3 us -> 43.1 us
    unnamed x21 -> x3, local copies, waits for them, and re-layouts: 9.99 us -> 4.36 us
    pallas_call x1, Pallas kernels: 44.3 us -> 43.1 us  [on_device(): pl.pallas_call(kernel, out_shape=(jax.ShapeDtypeStruct((FIELDS, PLANES, C...]
where the time goes in v2:
time: 48.9 us; the launch traced here: 48.7 us
  Pallas kernels  43.1 us (88%)
  local copies, waits for them, and re-layouts  4.36 us (9%)
  between operations  1.29 us (3%)
    pallas_call x1, Pallas kernels, on_device(): pl.pallas_call(kernel, out_shape=(jax.ShapeDtypeStruct((FIELDS, PLANES, C...  43.1 us
    unnamed x3, local copies, waits for them, and re-layouts  4.36 us

profile of v2, /device:TPU:1, one launch (start us, length us, event | category | flops | bytes accessed | tf_op | source)
XLA Modules:
  0.0 48.7 jit_solution(5314740805621989173)
XLA Ops:
  1.3 43.1 %sweep.1 = (f32[5,16,2048]{2,1,0:T(8,128)}, f32[3,128]{1,0:T(4,128)}, f32[5]{0:T(128)}) custom-call(f32[5,16,2048]{2,1,0:T(8,128)} %forcing.1, bf16[5,5,16,2048]{3,2,1,0:T(8,128)(2,1)} %inv_diag.1, bf16[5,5,16,2048]{3,2,1,0:T(8,128)(2,1)} %upper.1, s32[256]{0:T(256)} %cell.1, s32[1,256]{1,0:T(1,128)} %bitcast.3, s32[256]{0:T(256)} %slot.1, ...), custom_call_target="tpu_custom_call" | custom-call | flops 22000000 | bytes 4700000 | tf_op jit(solution)/shard_map/sweep/pallas_call | solution.py:506
  44.4 2.0 %copy.17 = f32[5,16,2048]{2,1,0:T(8,128)} copy(f32[5,16,2048]{2,1,0:T(8,128)} %get-tuple-element.6) | data formatting | bytes 1310720
  46.3 1.2 %copy.18 = f32[3,128]{1,0:T(4,128)} copy(f32[3,128]{1,0:T(4,128)} %get-tuple-element.7) | data formatting | bytes 3072
  47.6 1.1 %copy.19 = f32[5]{0:T(128)} copy(f32[5]{0:T(128)} %get-tuple-element.8) | data formatting | bytes 40

commit v3 on v2

--- a/solution.py
+++ b/solution.py
@@ -61,7 +61,7 @@
     aileron,
     fmap,
     arm,
-    adj_out,
+    adj,
     shell_out,
     hinge_out,
     f_v,
@@ -70,7 +70,6 @@
     cell_v,
     owner_v,
     slot_v,
-    count_s,
     ail_v,
     fmap_v,
     arm_v,
@@ -79,7 +78,6 @@
     maps_in,
     inc_out,
     inc_in,
-    adj,
     hot,
     msg,
     msg_in,
@@ -88,7 +86,6 @@
     hmsg_in,
     load_sem,
     small_sem,
-    out_sem,
     map_ssem,
     map_rsem,
     inc_ssem,
@@ -126,7 +123,6 @@
                 (cell, cell_v),
                 (owner, owner_v),
                 (slot, slot_v),
-                (count, count_s),
                 (aileron, ail_v),
                 (fmap, fmap_v),
                 (arm, arm_v),
@@ -256,7 +252,7 @@
         hot[pl.ds(c * LANES, LANES), :] = jnp.where(at == face_at, 1.0, 0.0).astype(jnp.bfloat16)
     plane_hit = lax.broadcasted_iota(jnp.int32, (PLANES, FACES), 0) == face_plane
     face_id = lax.broadcasted_iota(jnp.int32, (1, FACES), 1)
-    live = jnp.where(face_id < count_s[0], 1.0, 0.0)
+    live = jnp.where(face_id < count[0], 1.0, 0.0)
     owner_hot = jnp.where(
         lax.broadcasted_iota(jnp.int32, (NP, FACES), 0) == owner_v[...], 1.0, 0.0
     )
@@ -339,15 +335,6 @@
         return tuple(new)
 
     lax.fori_loop(0, PLANES, sweep, start)
-    outputs = []
-    for c in range(CHUNKS):
-        copy = pltpu.make_async_copy(
-            adj.at[:, pl.ds(c * ADJ_PITCH, PLANES), :],
-            adj_out.at[:, :, pl.ds(c * LANES, LANES)],
-            out_sem.at[c],
-        )
-        copy.start()
-        outputs.append(copy)
     gathered = jnp.zeros((2 * FIELDS * PLANES, FACES), jnp.float32)
     for c in range(0, CHUNKS, 2):
         pair = jnp.concatenate(
@@ -458,9 +445,6 @@
     for a in range(LOADS):
         shell_out[pl.ds(a, 1), :] = jnp.sum(loads[a], axis=0, keepdims=True)
 
-    for copy in outputs:
-        copy.wait()
-
     def sent(r, carry):
         peer = (me + r) % NS
         map_copy(0, peer, peer).wait_send()
@@ -483,8 +467,25 @@
         return carry
 
     lax.fori_loop(1, NS, wait_hinge, 0)
-    total = jnp.sum(hmsg_in[:, 0, :], axis=0) * (1.0 / math.sqrt(NS * NP * FACES))
-    hinge_out[...] = total[:FIELDS]
+    total = jnp.sum(hmsg_in[:, 0, :], axis=0, keepdims=True)
+    hinge_out[...] = total * (1.0 / math.sqrt(NS * NP * FACES))
+
+
+def store(adj, shell, hinge, adj_out, shell_out, hinge_out, sem):
+    copies = [
+        pltpu.make_async_copy(
+            adj.at[:, pl.ds(c * ADJ_PITCH, PLANES), :],
+            adj_out.at[:, :, pl.ds(c * LANES, LANES)],
+            sem.at[c],
+        )
+        for c in range(CHUNKS)
+    ]
+    for copy in copies:
+        copy.start()
+    shell_out[...] = shell[...]
+    hinge_out[...] = hinge[0, :FIELDS]
+    for copy in copies:
+        copy.wait()
 
 
 def on_device(
@@ -503,58 +504,7 @@
     vmem = pl.BlockSpec(memory_space=pltpu.VMEM)
     f32, bf16, i32 = jnp.float32, jnp.bfloat16, jnp.int32
     dma = pltpu.SemaphoreType.DMA
-    return pl.pallas_call(
-        kernel,
-        out_shape=(
-            jax.ShapeDtypeStruct((FIELDS, PLANES, CELLS), f32),
-            jax.ShapeDtypeStruct((LOADS, SHELL), f32),
-            jax.ShapeDtypeStruct((FIELDS,), f32),
-        ),
-        in_specs=[anywhere] * 10,
-        out_specs=(anywhere, vmem, vmem),
-        scratch_shapes=[
-            pltpu.VMEM((FIELDS, PLANES, CELLS), f32),
-            pltpu.VMEM((FIELDS, FIELDS, PLANES, CELLS), bf16),
-            pltpu.VMEM((FIELDS, FIELDS, PLANES, CELLS), bf16),
-            pltpu.VMEM((FACES,), i32),
-            pltpu.VMEM((1, FACES), i32),
-            pltpu.VMEM((FACES,), i32),
-            pltpu.SMEM((1,), i32),
-            pltpu.VMEM((FACES,), i32),
-            pltpu.VMEM((FIELDS, LOADS, FACES), f32),
-            pltpu.VMEM((FACES,), f32),
-            pltpu.VMEM((COMPS, CHUNKS * TERM_PITCH, LANES), f32),
-            pltpu.VMEM((CHUNKS * MAP_PITCH, LANES), f32),
-            pltpu.VMEM((NS * MAP_ROWS, LANES), f32),
-            pltpu.VMEM((NS * 8, LANES), f32),
-            pltpu.VMEM((CHUNKS * 8, LANES), f32),
-            pltpu.VMEM((FIELDS, CHUNKS * ADJ_PITCH, LANES), f32),
-            pltpu.VMEM((CELLS, FACES), bf16),
-            pltpu.VMEM((NP, 1, LANES), f32),
-            pltpu.VMEM((NP, 1, LANES), f32),
-            pltpu.VMEM((NP, LANES), f32),
-            pltpu.VMEM((1, 1, LANES), f32),
-            pltpu.VMEM((NS, 1, LANES), f32),
-            dma((GROUPS, 3)),
-            dma((7,)),
-            dma((CHUNKS,)),
-            dma((NS,)),
-            dma((NS,)),
-            dma((NS,)),
-            dma((NS,)),
-            dma((NP,)),
-            dma((NP,)),
-            dma((NS,)),
-            dma((NS,)),
-        ],
-        compiler_params=pltpu.CompilerParams(
-            collective_id=0, has_side_effects=True, vmem_limit_bytes=63 * 1024 * 1024
-        ),
-        cost_estimate=pl.CostEstimate(
-            flops=22_000_000, bytes_accessed=4_700_000, transcendentals=0
-        ),
-        name="sweep",
-    )(
+    operands = (
         forcing,
         inv_diag,
         upper_jac,
@@ -566,6 +516,74 @@
         jnp.swapaxes(face_map, 0, 1),
         hinge_arm,
     )
+    operands = [
+        x if x is face_count else pltpu.with_memory_space_constraint(x, pltpu.HBM)
+        for x in operands
+    ]
+    results = pl.pallas_call(
+        kernel,
+        out_shape=(
+            pltpu.VMEM((FIELDS, CHUNKS * ADJ_PITCH, LANES), f32),
+            pltpu.VMEM((LOADS, SHELL), f32),
+            pltpu.VMEM((1, LANES), f32),
+        ),
+        in_specs=[anywhere] * 6
+        + [pl.BlockSpec(memory_space=pltpu.SMEM)]
+        + [anywhere] * 3,
+        out_specs=(vmem, vmem, vmem),
+        scratch_shapes=[
+            pltpu.VMEM((FIELDS, PLANES, CELLS), f32),
+            pltpu.VMEM((FIELDS, FIELDS, PLANES, CELLS), bf16),
+            pltpu.VMEM((FIELDS, FIELDS, PLANES, CELLS), bf16),
+            pltpu.VMEM((FACES,), i32),
+            pltpu.VMEM((1, FACES), i32),
+            pltpu.VMEM((FACES,), i32),
+            pltpu.VMEM((FACES,), i32),
+            pltpu.VMEM((FIELDS, LOADS, FACES), f32),
+            pltpu.VMEM((FACES,), f32),
+            pltpu.VMEM((COMPS, CHUNKS * TERM_PITCH, LANES), f32),
+            pltpu.VMEM((CHUNKS * MAP_PITCH, LANES), f32),
+            pltpu.VMEM((NS * MAP_ROWS, LANES), f32),
+            pltpu.VMEM((NS * 8, LANES), f32),
+            pltpu.VMEM((CHUNKS * 8, LANES), f32),
+            pltpu.VMEM((CELLS, FACES), bf16),
+            pltpu.VMEM((NP, 1, LANES), f32),
+            pltpu.VMEM((NP, 1, LANES), f32),
+            pltpu.VMEM((NP, LANES), f32),
+            pltpu.VMEM((1, 1, LANES), f32),
+            pltpu.VMEM((NS, 1, LANES), f32),
+            dma((GROUPS, 3)),
+            dma((6,)),
+            dma((NS,)),
+            dma((NS,)),
+            dma((NS,)),
+            dma((NS,)),
+            dma((NP,)),
+            dma((NP,)),
+            dma((NS,)),
+            dma((NS,)),
+        ],
+        compiler_params=pltpu.CompilerParams(
+            collective_id=0, has_side_effects=True, vmem_limit_bytes=40 * 1024 * 1024
+        ),
+        cost_estimate=pl.CostEstimate(
+            flops=22_000_000, bytes_accessed=4_700_000, transcendentals=0
+        ),
+        name="sweep",
+    )(*operands)
+    return pl.pallas_call(
+        store,
+        out_shape=(
+            jax.ShapeDtypeStruct((FIELDS, PLANES, CELLS), f32),
+            jax.ShapeDtypeStruct((LOADS, SHELL), f32),
+            jax.ShapeDtypeStruct((FIELDS,), f32),
+        ),
+        in_specs=[vmem] * 3,
+        out_specs=(anywhere, vmem, vmem),
+        scratch_shapes=[dma((CHUNKS,))],
+        compiler_params=pltpu.CompilerParams(vmem_limit_bytes=16 * 1024 * 1024),
+        name="store",
+    )(*results)
 
 
 def solution(mesh):

time: 48.9 us -> 45.3 us (0.926)
  local copies, waits for them, and re-layouts: 4.36 us -> 0 us
  Pallas kernels: 43.1 us -> 43.8 us
    unnamed x3 -> x0, local copies, waits for them, and re-layouts: 4.36 us -> none
    pallas_call x1 -> x2, Pallas kernels: 43.1 us -> 43.8 us  [the longest x1 42.3 us: on_device(): pl.pallas_call(kernel, out_shape=(pltpu.VMEM((FIELDS, CHUNKS * ADJ_PITCH,...]
where the time goes in v3:
time: 45.3 us; the launch traced here: 45.1 us
  Pallas kernels  43.8 us (97%)
  between operations  1.29 us (3%)
    pallas_call x1, Pallas kernels, on_device(): pl.pallas_call(kernel, out_shape=(pltpu.VMEM((FIELDS, CHUNKS * ADJ_PITCH,...  42.3 us
    pallas_call x1, Pallas kernels, on_device(): pl.pallas_call(store, out_shape=(jax.ShapeDtypeStruct((FIELDS, PLANES, CE...  1.54 us

profile of v3, /device:TPU:1, one launch (start us, length us, event | category | flops | bytes accessed | tf_op | source)
XLA Modules:
  0.0 45.1 jit_solution(919139855912687036)
XLA Ops:
  1.3 42.3 %sweep.1 = (f32[5,384,128]{2,1,0:T(8,128)S(1)}, f32[3,128]{1,0:T(4,128)S(1)}, f32[1,128]{1,0:T(1,128)S(1)}) custom-call(f32[5,16,2048]{2,1,0:T(8,128)} %forcing.1, bf16[5,5,16,2048]{3,2,1,0:T(8,128)(2,1)} %inv_diag.1, bf16[5,5,16,2048]{3,2,1,0:T(8,128)(2,1)} %upper.1, s32[256]{0:T(256)} %cell.1, s32[1,256]{1,0:T(1,128)} %bitcast.3, s32[256]{0:T(256)} %slot.1, ...), custom_call_target="tpu_custom_call" | custom-call | flops 22000000 | bytes 4700000 | tf_op jit(solution)/shard_map/sweep/pallas_call | solution.py:523
  43.6 1.5 %store.1 = (f32[5,16,2048]{2,1,0:T(8,128)}, f32[3,128]{1,0:T(4,128)}, f32[5]{0:T(128)}) custom-call(f32[5,384,128]{2,1,0:T(8,128)S(1)} %get-tuple-element.6.adj, f32[3,128]{1,0:T(4,128)S(1)} %get-tuple-element.7.shell, f32[1,128]{1,0:T(1,128)S(1)} %get-tuple-element.8.hinge), custom_call_target="tpu_custom_call" | custom-call | tf_op jit(solution)/shard_map/store/pallas_call | solution.py:574

commit v4 on v3

--- a/solution.py
+++ b/solution.py
@@ -29,9 +29,8 @@
 GROUPS = 4
 GROUP_CELLS = CELLS // GROUPS
 GROUP_CHUNKS = CHUNKS // GROUPS
-HINGE_AT = 0
-LOAD_AT = 16
-SLOT_AT = 64
+LOAD_AT = 0
+SLOT_AT = 48
 
 
 def chunk_of(dev):
@@ -74,24 +73,34 @@
     fmap_v,
     arm_v,
     terms,
+    prefix,
+    weights,
     maps,
     maps_in,
+    gains,
+    gains_in,
     inc_out,
     inc_in,
     hot,
     msg,
     msg_in,
     rows_in,
+    zmsg,
+    zmsg_in,
     hmsg,
     hmsg_in,
     load_sem,
     small_sem,
     map_ssem,
     map_rsem,
+    gain_ssem,
+    gain_rsem,
     inc_ssem,
     inc_rsem,
     face_ssem,
     face_rsem,
+    z_ssem,
+    z_rsem,
     hinge_ssem,
     hinge_rsem,
 ):
@@ -113,9 +122,6 @@
             ),
         )
 
-    for g in range(GROUPS):
-        for copy in load_copies(g):
-            copy.start()
     small = [
         pltpu.make_async_copy(src, dst, small_sem.at[n])
         for n, (src, dst) in enumerate(
@@ -131,6 +137,9 @@
     ]
     for copy in small:
         copy.start()
+    for g in range(GROUPS):
+        for copy in load_copies(g):
+            copy.start()
 
     def greet_span(r, carry):
         pl.semaphore_signal(
@@ -147,6 +156,43 @@
     lax.fori_loop(1, NS, greet_span, 0)
     lax.fori_loop(1, NP, greet_plane, 0)
     inc_out[...] = jnp.zeros_like(inc_out)
+
+    def by_face(left, right):
+        return lax.dot_general(
+            left, right, (((1,), (1,)), ((), ())), preferred_element_type=jnp.float32
+        )
+
+    for copy in small:
+        copy.wait()
+    face_cell = cell_v[...].reshape(1, FACES)
+    face_plane = face_cell // CELLS
+    face_at = face_cell % CELLS
+    for c in range(CHUNKS):
+        at = lax.broadcasted_iota(jnp.int32, (LANES, FACES), 0) + c * LANES
+        hot[pl.ds(c * LANES, LANES), :] = jnp.where(at == face_at, 1.0, 0.0).astype(jnp.bfloat16)
+    plane_hit = lax.broadcasted_iota(jnp.int32, (PLANES, FACES), 0) == face_plane
+    face_id = lax.broadcasted_iota(jnp.int32, (1, FACES), 1)
+    live = jnp.where(face_id < count[0], 1.0, 0.0)
+    owner_hot = jnp.where(
+        lax.broadcasted_iota(jnp.int32, (NP, FACES), 0) == owner_v[...], 1.0, 0.0
+    )
+    owner_hot16 = owner_hot.astype(jnp.bfloat16)
+    earlier = jnp.where(
+        lax.broadcasted_iota(jnp.int32, (FACES, FACES), 0)
+        < lax.broadcasted_iota(jnp.int32, (FACES, FACES), 1),
+        1.0,
+        0.0,
+    ).astype(jnp.bfloat16)
+    before = jnp.dot(owner_hot16, earlier, preferred_element_type=jnp.float32)
+    rank = jnp.sum(owner_hot * before, axis=0, keepdims=True).astype(jnp.int32)
+    rank_hot = jnp.where(lax.broadcasted_iota(jnp.int32, (CAP, FACES), 0) == rank, 1.0, 0.0)
+    slot_value = (slot_v[...].reshape(1, FACES) + 1).astype(jnp.float32) * live
+    slot_rows = rank_hot * slot_value
+    weight = ail_v[...].reshape(1, FACES).astype(jnp.float32) * live * arm_v[...].reshape(1, FACES)
+    at_plane = jnp.where(plane_hit, weight, 0.0)
+    for c in range(CHUNKS):
+        spread = by_face(jnp.concatenate(split(at_plane), axis=0), hot[pl.ds(c * LANES, LANES), :])
+        weights[pl.ds(c * TERM_PITCH, PLANES), :] = spread[:PLANES] + spread[PLANES:]
 
     def chunk_terms(c, carry):
         cells = pl.ds(pl.multiple_of(c * LANES, LANES), LANES)
@@ -181,8 +227,13 @@
             out.append(total if start is None else total + start[i])
         return out
 
+    def prefix_rows(half, k):
+        return pl.ds(pl.multiple_of((k * 2 + half) * HALF, HALF), HALF)
+
     def section_map(half):
         state = tuple(term(n, half, PLANES - 1) for n in range(COMPS))
+        for n in range(COMPS):
+            prefix[n, prefix_rows(half, PLANES - 1), :] = state[n]
 
         def compose(step, state):
             k = PLANES - 2 - step
@@ -194,6 +245,8 @@
                 for i in range(FIELDS):
                     new[i * FIELDS + col] = column[i]
             new[FIELDS * FIELDS :] = matvec(coupling, state[FIELDS * FIELDS :], source)
+            for n in range(COMPS):
+                prefix[n, prefix_rows(half, k), :] = new[n]
             return tuple(new)
 
         state = lax.fori_loop(0, PLANES - 1, compose, state)
@@ -216,6 +269,18 @@
             device_id_type=MESH,
         )
 
+    def gain_copy(c, dest, source):
+        return pltpu.make_async_remote_copy(
+            src_ref=gains.at[out_rows(c), :],
+            dst_ref=gains_in.at[map_rows(source), :],
+            send_sem=gain_ssem.at[dest],
+            recv_sem=gain_rsem.at[source],
+            device_id=(dest, q),
+            device_id_type=MESH,
+        )
+
+    for n in range(FIELDS * FIELDS, MAP_ROWS):
+        gains[pl.ds(n, CHUNKS, stride=MAP_PITCH), :] = jnp.zeros((CHUNKS, LANES), jnp.float32)
     for n in range(COMPS, MAP_ROWS):
         maps[pl.ds(n, CHUNKS, stride=MAP_PITCH), :] = jnp.zeros((CHUNKS, LANES), jnp.float32)
 
@@ -242,33 +307,28 @@
 
         lax.fori_loop(0, HALF, send_map, 0)
 
-    for copy in small:
-        copy.wait()
-    face_cell = cell_v[...].reshape(1, FACES)
-    face_plane = face_cell // CELLS
-    face_at = face_cell % CELLS
-    for c in range(CHUNKS):
-        at = lax.broadcasted_iota(jnp.int32, (LANES, FACES), 0) + c * LANES
-        hot[pl.ds(c * LANES, LANES), :] = jnp.where(at == face_at, 1.0, 0.0).astype(jnp.bfloat16)
-    plane_hit = lax.broadcasted_iota(jnp.int32, (PLANES, FACES), 0) == face_plane
-    face_id = lax.broadcasted_iota(jnp.int32, (1, FACES), 1)
-    live = jnp.where(face_id < count[0], 1.0, 0.0)
-    owner_hot = jnp.where(
-        lax.broadcasted_iota(jnp.int32, (NP, FACES), 0) == owner_v[...], 1.0, 0.0
-    )
-    owner_hot16 = owner_hot.astype(jnp.bfloat16)
-    earlier = jnp.where(
-        lax.broadcasted_iota(jnp.int32, (FACES, FACES), 0)
-        < lax.broadcasted_iota(jnp.int32, (FACES, FACES), 1),
-        1.0,
-        0.0,
-    ).astype(jnp.bfloat16)
-    before = jnp.dot(owner_hot16, earlier, preferred_element_type=jnp.float32)
-    rank = jnp.sum(owner_hot * before, axis=0, keepdims=True).astype(jnp.int32)
-    rank_hot = jnp.where(lax.broadcasted_iota(jnp.int32, (CAP, FACES), 0) == rank, 1.0, 0.0)
-    slot_value = (slot_v[...].reshape(1, FACES) + 1).astype(jnp.float32) * live
-    slot_rows = rank_hot * slot_value
-    weight = ail_v[...].reshape(1, FACES).astype(jnp.float32) * live * arm_v[...].reshape(1, FACES)
+    constant = [jnp.zeros((HALF, LANES), jnp.float32) for _ in range(FIELDS)]
+    for half in range(2):
+
+        def add_plane(k, total):
+            weight_k = weights[pl.ds(half * HALF * TERM_PITCH + k, HALF, stride=TERM_PITCH), :]
+            return tuple(
+                total[n] + weight_k * prefix[n, prefix_rows(half, k), :] for n in range(COMPS)
+            )
+
+        zero = jnp.zeros((HALF, LANES), jnp.float32)
+        total = lax.fori_loop(0, PLANES, add_plane, (zero,) * COMPS)
+        for n in range(FIELDS * FIELDS):
+            gains[pl.ds(half * HALF * MAP_PITCH + n, HALF, stride=MAP_PITCH), :] = total[n]
+        constant = [constant[i] + total[FIELDS * FIELDS + i] for i in range(FIELDS)]
+
+    def send_gain(r, carry):
+        dest = (me + r) % NS
+        gain_copy(chunk_of(dest), dest, me).start()
+        return carry
+
+    lax.fori_loop(1, NS, send_gain, 0)
+    gains_in[map_rows(me), :] = gains[out_rows(my_chunk), :]
 
     maps_in[map_rows(me), :] = maps[out_rows(my_chunk), :]
     vec = [jnp.zeros((1, LANES), jnp.float32) for _ in range(FIELDS)]
@@ -308,6 +368,49 @@
     inc_in[pl.ds(pl.multiple_of(my_chunk * 8, 8), 8), :] = inc_out[
         pl.ds(pl.multiple_of(me * 8, 8), 8), :
     ]
+
+    def wait_gain(r, carry):
+        peer = (me + r) % NS
+        gain_copy(0, peer, peer).wait_recv()
+        return carry
+
+    lax.fori_loop(1, NS, wait_gain, 0)
+    partial = constant
+    for section in range(NS - 1):
+        entering = inc_out[pl.ds(section * 8, 8), :]
+        partial = [
+            partial[i]
+            + gains_in[pl.ds(section * MAP_ROWS + i * FIELDS, 8), :] * entering
+            for i in range(FIELDS)
+        ]
+    columns = jnp.concatenate(
+        [jnp.sum(partial[i], axis=0, keepdims=True) for i in range(FIELDS)]
+        + [jnp.zeros((8 - FIELDS, LANES), jnp.float32)],
+        axis=0,
+    )
+    diagonal = lax.broadcasted_iota(jnp.int32, (8, LANES), 0) == lax.broadcasted_iota(
+        jnp.int32, (8, LANES), 1
+    )
+    zmsg[0] = jnp.sum(
+        jnp.where(diagonal, jnp.sum(columns, axis=1, keepdims=True), 0.0), axis=0, keepdims=True
+    )
+
+    def z_copy(dest, source):
+        return pltpu.make_async_remote_copy(
+            src_ref=zmsg.at[0],
+            dst_ref=zmsg_in.at[source],
+            send_sem=z_ssem.at[dest],
+            recv_sem=z_rsem.at[source],
+            device_id=(me, dest),
+            device_id_type=MESH,
+        )
+
+    def send_z(r, carry):
+        z_copy((q + r) % NP, q).start()
+        return carry
+
+    lax.fori_loop(1, NP, send_z, 0)
+    zmsg_in[q] = zmsg[0]
 
     for half in range(2):
         for j in range(HALF):
@@ -363,29 +466,15 @@
         for i in range(1, FIELDS):
             total = total + fmap_v[i, pl.ds(a, 1), :] * rows[i]
         load_rows.append(rank_hot * (total * live))
-    hinge_rows = jnp.concatenate(
-        [rows[i] * weight for i in range(FIELDS)]
-        + [jnp.zeros((LANES - FIELDS, FACES), jnp.float32)],
-        axis=0,
-    )
     face_rows = jnp.concatenate(
-        [jnp.zeros((LOAD_AT, FACES), jnp.float32)]
-        + load_rows
+        load_rows
         + [slot_rows, jnp.zeros((LANES - SLOT_AT - CAP, FACES), jnp.float32)],
         axis=0,
     )
 
-    def by_face(left, right):
-        return lax.dot_general(
-            left, right, (((1,), (1,)), ((), ())), preferred_element_type=jnp.float32
-        )
-
-    every = jnp.ones((NP, FACES), jnp.bfloat16)
     packed = jnp.zeros((NP, LANES), jnp.float32)
     for piece in split(face_rows):
         packed = packed + by_face(owner_hot16, piece)
-    for piece in split(hinge_rows):
-        packed = packed + by_face(every, piece)
     msg[:, 0, :] = packed
 
     def face_copy(dest, source):
@@ -405,17 +494,13 @@
     lax.fori_loop(1, NP, send_face, 0)
     msg_in[q] = msg[q]
 
-    def wait_face(r, carry):
+    def wait_z(r, carry):
         peer = (q + r) % NP
-        face_copy(peer, peer).wait_recv()
-        return carry
-
-    lax.fori_loop(1, NP, wait_face, 0)
-    for peer in range(NP):
-        rows_in[pl.ds(peer, 1), :] = msg_in[peer]
-    arrived = rows_in[...]
-
-    hmsg[0] = jnp.sum(arrived, axis=0, keepdims=True)
+        z_copy(peer, peer).wait_recv()
+        return carry
+
+    lax.fori_loop(1, NP, wait_z, 0)
+    hmsg[0] = jnp.sum(zmsg_in[...], axis=0)
 
     def hinge_copy(dest, source):
         return pltpu.make_async_remote_copy(
@@ -433,6 +518,16 @@
 
     lax.fori_loop(1, NS, send_hinge, 0)
     hmsg_in[me] = hmsg[0]
+
+    def wait_face(r, carry):
+        peer = (q + r) % NP
+        face_copy(peer, peer).wait_recv()
+        return carry
+
+    lax.fori_loop(1, NP, wait_face, 0)
+    for peer in range(NP):
+        rows_in[pl.ds(peer, 1), :] = msg_in[peer]
+    arrived = rows_in[...]
 
     lane = lax.broadcasted_iota(jnp.int32, (NP, LANES), 1) + 1
     loads = [jnp.zeros((NP, SHELL), jnp.float32) for _ in range(LOADS)]
@@ -448,6 +543,7 @@
     def sent(r, carry):
         peer = (me + r) % NS
         map_copy(0, peer, peer).wait_send()
+        gain_copy(0, peer, peer).wait_send()
         inc_copy(peer, 0, peer).wait_send()
         return carry
 
@@ -456,6 +552,7 @@
     def sent_face(r, carry):
         peer = (q + r) % NP
         face_copy(peer, peer).wait_send()
+        z_copy(peer, peer).wait_send()
         return carry
 
     lax.fori_loop(1, NP, sent_face, 0)
@@ -542,6 +639,10 @@
             pltpu.VMEM((FIELDS, LOADS, FACES), f32),
             pltpu.VMEM((FACES,), f32),
             pltpu.VMEM((COMPS, CHUNKS * TERM_PITCH, LANES), f32),
+            pltpu.VMEM((COMPS, 2 * PLANES * HALF, LANES), f32),
+            pltpu.VMEM((CHUNKS * TERM_PITCH, LANES), f32),
+            pltpu.VMEM((CHUNKS * MAP_PITCH, LANES), f32),
+            pltpu.VMEM((NS * MAP_ROWS, LANES), f32),
             pltpu.VMEM((CHUNKS * MAP_PITCH, LANES), f32),
             pltpu.VMEM((NS * MAP_ROWS, LANES), f32),
             pltpu.VMEM((NS * 8, LANES), f32),
@@ -551,6 +652,8 @@
             pltpu.VMEM((NP, 1, LANES), f32),
             pltpu.VMEM((NP, LANES), f32),
             pltpu.VMEM((1, 1, LANES), f32),
+            pltpu.VMEM((NP, 1, LANES), f32),
+            pltpu.VMEM((1, 1, LANES), f32),
             pltpu.VMEM((NS, 1, LANES), f32),
             dma((GROUPS, 3)),
             dma((6,)),
@@ -558,6 +661,10 @@
             dma((NS,)),
             dma((NS,)),
             dma((NS,)),
+            dma((NS,)),
+            dma((NS,)),
+            dma((NP,)),
+            dma((NP,)),
             dma((NP,)),
             dma((NP,)),
             dma((NS,)),

time: 45.3 us -> 45.1 us (level)
  no operation moved by 1% of the time
where the time goes in v4:
time: 45.1 us; the launch traced here: 45 us
  Pallas kernels  43.7 us (97%)
  between operations  1.29 us (3%)
    pallas_call x1, Pallas kernels, on_device(): pl.pallas_call(kernel, out_shape=(pltpu.VMEM((FIELDS, CHUNKS * ADJ_PITCH,...  42.1 us
    pallas_call x1, Pallas kernels, on_device(): pl.pallas_call(store, out_shape=(jax.ShapeDtypeStruct((FIELDS, PLANES, CE...  1.54 us

profile of v4, /device:TPU:1, one launch (start us, length us, event | category | flops | bytes accessed | tf_op | source)
XLA Modules:
  0.0 45.0 jit_solution(8612456234001672396)
XLA Ops:
  1.3 42.1 %sweep.1 = (f32[5,384,128]{2,1,0:T(8,128)S(1)}, f32[3,128]{1,0:T(4,128)S(1)}, f32[1,128]{1,0:T(1,128)S(1)}) custom-call(f32[5,16,2048]{2,1,0:T(8,128)} %forcing.1, bf16[5,5,16,2048]{3,2,1,0:T(8,128)(2,1)} %inv_diag.1, bf16[5,5,16,2048]{3,2,1,0:T(8,128)(2,1)} %upper.1, s32[256]{0:T(256)} %cell.1, s32[1,256]{1,0:T(1,128)} %bitcast.3, s32[256]{0:T(256)} %slot.1, ...), custom_call_target="tpu_custom_call" | custom-call | flops 22000000 | bytes 4700000 | tf_op jit(solution)/shard_map/sweep/pallas_call | solution.py:620
  43.4 1.5 %store.1 = (f32[5,16,2048]{2,1,0:T(8,128)}, f32[3,128]{1,0:T(4,128)}, f32[5]{0:T(128)}) custom-call(f32[5,384,128]{2,1,0:T(8,128)S(1)} %get-tuple-element.6.adj, f32[3,128]{1,0:T(4,128)S(1)} %get-tuple-element.7.shell, f32[1,128]{1,0:T(1,128)S(1)} %get-tuple-element.8.hinge), custom_call_target="tpu_custom_call" | custom-call | tf_op jit(solution)/shard_map/store/pallas_call | solution.py:681

commit v5 on v3

--- a/solution.py
+++ b/solution.py
@@ -84,6 +84,7 @@
     rows_in,
     hmsg,
     hmsg_in,
+    ready,
     load_sem,
     small_sem,
     map_ssem,
@@ -138,15 +139,37 @@
         )
         return carry
 
-    def greet_plane(r, carry):
-        pl.semaphore_signal(
-            barrier, inc=1, device_id=(me, (q + r) % NP), device_id_type=MESH
-        )
-        return carry
-
+    depth, core = q // 2, q % 2
+
+    def along(distance, other=0):
+        return (me, ((depth + distance) % (NP // 2)) * 2 + (core + other) % 2)
+
+    near = [along(0, 1)] + [along(d, other) for d in (1, -1) for other in (0, 1)]
+    for peer in near:
+        pl.semaphore_signal(barrier, inc=1, device_id=peer, device_id_type=MESH)
     lax.fori_loop(1, NS, greet_span, 0)
-    lax.fori_loop(1, NP, greet_plane, 0)
+
+    def tell(step):
+        for d in (1 << step, -(1 << step)):
+            pl.semaphore_signal(
+                ready.at[step], inc=1, device_id=along(d), device_id_type=MESH
+            )
+
+    def hear(step):
+        pl.semaphore_wait(ready.at[step], 2)
+
     inc_out[...] = jnp.zeros_like(inc_out)
+
+    def everything(ref, count, send_sem, recv_sem, peer):
+        whole = ref.at[pl.ds(0, count)]
+        return pltpu.make_async_remote_copy(
+            src_ref=whole,
+            dst_ref=whole,
+            send_sem=send_sem,
+            recv_sem=recv_sem,
+            device_id=peer,
+            device_id_type=MESH,
+        )
 
     def chunk_terms(c, carry):
         cells = pl.ds(pl.multiple_of(c * LANES, LANES), LANES)
@@ -210,8 +233,8 @@
         return pltpu.make_async_remote_copy(
             src_ref=maps.at[out_rows(c), :],
             dst_ref=maps_in.at[map_rows(source), :],
-            send_sem=map_ssem.at[dest],
-            recv_sem=map_rsem.at[source],
+            send_sem=map_ssem,
+            recv_sem=map_rsem,
             device_id=(dest, q),
             device_id_type=MESH,
         )
@@ -228,7 +251,8 @@
             lax.fori_loop(g * GROUP_CHUNKS, (g + 1) * GROUP_CHUNKS, chunk_terms, 0)
         section_map(half)
         if half == 0:
-            pl.semaphore_wait(barrier, NS - 1 + NP - 1)
+            pl.semaphore_wait(barrier, NS - 1 + len(near))
+            tell(0)
 
         def send_map(t, carry):
             j = (my_j + t) % HALF
@@ -241,6 +265,9 @@
             return carry
 
         lax.fori_loop(0, HALF, send_map, 0)
+
+    hear(0)
+    tell(1)
 
     for copy in small:
         copy.wait()
@@ -270,13 +297,14 @@
     slot_rows = rank_hot * slot_value
     weight = ail_v[...].reshape(1, FACES).astype(jnp.float32) * live * arm_v[...].reshape(1, FACES)
 
+    hear(1)
+    tell(2)
+
+    all_maps = everything(maps_in, (NS - 1) * MAP_ROWS, map_ssem, map_rsem, near[0])
+    all_maps.wait_recv()
     maps_in[map_rows(me), :] = maps[out_rows(my_chunk), :]
     vec = [jnp.zeros((1, LANES), jnp.float32) for _ in range(FIELDS)]
     for section in range(NS - 1, 0, -1):
-
-        @pl.when(me != section)
-        def _():
-            map_copy(0, section, section).wait_recv()
 
         def entry(n):
             return maps_in[pl.ds(section * MAP_ROWS + n, 1), :]
@@ -286,16 +314,12 @@
         for i in range(FIELDS):
             inc_out[pl.ds((section - 1) * 8 + i, 1), :] = vec[i]
 
-    @pl.when(me != 0)
-    def _():
-        map_copy(0, 0, 0).wait_recv()
-
     def inc_copy(dest, c, source):
         return pltpu.make_async_remote_copy(
             src_ref=inc_out.at[pl.ds(pl.multiple_of(dest * 8, 8), 8), :],
             dst_ref=inc_in.at[pl.ds(pl.multiple_of(c * 8, 8), 8), :],
-            send_sem=inc_ssem.at[dest],
-            recv_sem=inc_rsem.at[source],
+            send_sem=inc_ssem,
+            recv_sem=inc_rsem,
             device_id=(dest, q),
             device_id_type=MESH,
         )
@@ -305,17 +329,11 @@
         return carry
 
     lax.fori_loop(1, NS, send_inc, 0)
+    all_inc = everything(inc_in, (NS - 1) * 8, inc_ssem, inc_rsem, near[0])
+    all_inc.wait_recv()
     inc_in[pl.ds(pl.multiple_of(my_chunk * 8, 8), 8), :] = inc_out[
         pl.ds(pl.multiple_of(me * 8, 8), 8), :
     ]
-
-    for half in range(2):
-        for j in range(HALF):
-            dev = device_of(half, j)
-
-            @pl.when(me != dev)
-            def _():
-                inc_copy(dev, half * HALF + j, dev).wait_recv()
 
     start = tuple(
         tuple(inc_in[pl.ds(half * HALF * 8 + i, HALF, stride=8), :] for i in range(FIELDS))
@@ -392,25 +410,22 @@
         return pltpu.make_async_remote_copy(
             src_ref=msg.at[dest],
             dst_ref=msg_in.at[source],
-            send_sem=face_ssem.at[dest],
-            recv_sem=face_rsem.at[source],
+            send_sem=face_ssem,
+            recv_sem=face_rsem,
             device_id=(me, dest),
             device_id_type=MESH,
         )
+
+    hear(2)
 
     def send_face(r, carry):
         face_copy((q + r) % NP, q).start()
         return carry
 
     lax.fori_loop(1, NP, send_face, 0)
+    all_faces = everything(msg_in, NP - 1, face_ssem, face_rsem, near[0])
+    all_faces.wait_recv()
     msg_in[q] = msg[q]
-
-    def wait_face(r, carry):
-        peer = (q + r) % NP
-        face_copy(peer, peer).wait_recv()
-        return carry
-
-    lax.fori_loop(1, NP, wait_face, 0)
     for peer in range(NP):
         rows_in[pl.ds(peer, 1), :] = msg_in[peer]
     arrived = rows_in[...]
@@ -421,8 +436,8 @@
         return pltpu.make_async_remote_copy(
             src_ref=hmsg.at[0],
             dst_ref=hmsg_in.at[source],
-            send_sem=hinge_ssem.at[dest],
-            recv_sem=hinge_rsem.at[source],
+            send_sem=hinge_ssem,
+            recv_sem=hinge_rsem,
             device_id=(dest, q),
             device_id_type=MESH,
         )
@@ -432,7 +447,6 @@
         return carry
 
     lax.fori_loop(1, NS, send_hinge, 0)
-    hmsg_in[me] = hmsg[0]
 
     lane = lax.broadcasted_iota(jnp.int32, (NP, LANES), 1) + 1
     loads = [jnp.zeros((NP, SHELL), jnp.float32) for _ in range(LOADS)]
@@ -445,46 +459,32 @@
     for a in range(LOADS):
         shell_out[pl.ds(a, 1), :] = jnp.sum(loads[a], axis=0, keepdims=True)
 
-    def sent(r, carry):
-        peer = (me + r) % NS
-        map_copy(0, peer, peer).wait_send()
-        inc_copy(peer, 0, peer).wait_send()
-        return carry
-
-    lax.fori_loop(1, NS, sent, 0)
-
-    def sent_face(r, carry):
-        peer = (q + r) % NP
-        face_copy(peer, peer).wait_send()
-        return carry
-
-    lax.fori_loop(1, NP, sent_face, 0)
-
-    def wait_hinge(r, carry):
-        peer = (me + r) % NS
-        hinge_copy(peer, peer).wait_send()
-        hinge_copy(peer, peer).wait_recv()
-        return carry
-
-    lax.fori_loop(1, NS, wait_hinge, 0)
-    total = jnp.sum(hmsg_in[:, 0, :], axis=0, keepdims=True)
-    hinge_out[...] = total * (1.0 / math.sqrt(NS * NP * FACES))
-
-
-def store(adj, shell, hinge, adj_out, shell_out, hinge_out, sem):
-    copies = [
+    all_maps.wait_send()
+    all_inc.wait_send()
+    all_faces.wait_send()
+    all_hinge = everything(hmsg_in, NS - 1, hinge_ssem, hinge_rsem, near[0])
+    all_hinge.wait_send()
+    all_hinge.wait_recv()
+    hmsg_in[me] = hmsg[0]
+    total = jnp.sum(hmsg_in[:, 0, :], axis=0) * (1.0 / math.sqrt(NS * NP * FACES))
+    hinge_out[...] = total[:FIELDS]
+
+
+def store(adj, shell, hinge, adj_out, shell_out, hinge_out, adj_sem, shell_sem, hinge_sem):
+    for c in range(CHUNKS):
         pltpu.make_async_copy(
             adj.at[:, pl.ds(c * ADJ_PITCH, PLANES), :],
             adj_out.at[:, :, pl.ds(c * LANES, LANES)],
-            sem.at[c],
-        )
-        for c in range(CHUNKS)
-    ]
-    for copy in copies:
+            adj_sem,
+        ).start()
+    rest = (
+        pltpu.make_async_copy(shell, shell_out, shell_sem),
+        pltpu.make_async_copy(hinge, hinge_out, hinge_sem),
+    )
+    for copy in rest:
         copy.start()
-    shell_out[...] = shell[...]
-    hinge_out[...] = hinge[0, :FIELDS]
-    for copy in copies:
+    pltpu.make_async_copy(adj_out, adj_out, adj_sem).wait()
+    for copy in rest:
         copy.wait()
 
 
@@ -525,7 +525,7 @@
         out_shape=(
             pltpu.VMEM((FIELDS, CHUNKS * ADJ_PITCH, LANES), f32),
             pltpu.VMEM((LOADS, SHELL), f32),
-            pltpu.VMEM((1, LANES), f32),
+            pltpu.VMEM((FIELDS,), f32),
         ),
         in_specs=[anywhere] * 6
         + [pl.BlockSpec(memory_space=pltpu.SMEM)]
@@ -552,17 +552,11 @@
             pltpu.VMEM((NP, LANES), f32),
             pltpu.VMEM((1, 1, LANES), f32),
             pltpu.VMEM((NS, 1, LANES), f32),
+            pltpu.SemaphoreType.REGULAR((3,)),
             dma((GROUPS, 3)),
             dma((6,)),
-            dma((NS,)),
-            dma((NS,)),
-            dma((NS,)),
-            dma((NS,)),
-            dma((NP,)),
-            dma((NP,)),
-            dma((NS,)),
-            dma((NS,)),
-        ],
+        ]
+        + [dma] * 8,
         compiler_params=pltpu.CompilerParams(
             collective_id=0, has_side_effects=True, vmem_limit_bytes=40 * 1024 * 1024
         ),
@@ -579,8 +573,8 @@
             jax.ShapeDtypeStruct((FIELDS,), f32),
         ),
         in_specs=[vmem] * 3,
-        out_specs=(anywhere, vmem, vmem),
-        scratch_shapes=[dma((CHUNKS,))],
+        out_specs=[anywhere] * 3,
+        scratch_shapes=[dma] * 3,
         compiler_params=pltpu.CompilerParams(vmem_limit_bytes=16 * 1024 * 1024),
         name="store",
     )(*results)

time: 45.3 us -> 41.6 us (0.918)
  Pallas kernels: 43.8 us -> 40.2 us
    pallas_call x1, Pallas kernels: 42.3 us -> 39.3 us  [on_device(): pl.pallas_call(kernel, out_shape=(pltpu.VMEM((FIELDS, CHUNKS * ADJ_PITCH,...]
    pallas_call x1, Pallas kernels: 1.54 us -> 0.85 us  [on_device(): pl.pallas_call(store, out_shape=(jax.ShapeDtypeStruct((FIELDS, PLANES, CE...]
where the time goes in v5:
time: 41.6 us; the launch traced here: 41.5 us
  Pallas kernels  40.2 us (97%)
  between operations  1.29 us (3%)
    pallas_call x1, Pallas kernels, on_device(): pl.pallas_call(kernel, out_shape=(pltpu.VMEM((FIELDS, CHUNKS * ADJ_PITCH,...  39.3 us
    pallas_call x1, Pallas kernels, on_device(): pl.pallas_call(store, out_shape=(jax.ShapeDtypeStruct((FIELDS, PLANES, CE...  0.85 us

profile of v5, /device:TPU:1, one launch (start us, length us, event | category | flops | bytes accessed | tf_op | source)
XLA Modules:
  0.0 41.5 jit_solution(10961962445922223272)
XLA Ops:
  1.3 39.3 %sweep.1 = (f32[5,384,128]{2,1,0:T(8,128)S(1)}, f32[3,128]{1,0:T(4,128)S(1)}, f32[5]{0:T(128)S(1)}) custom-call(f32[5,16,2048]{2,1,0:T(8,128)} %forcing.1, bf16[5,5,16,2048]{3,2,1,0:T(8,128)(2,1)} %inv_diag.1, bf16[5,5,16,2048]{3,2,1,0:T(8,128)(2,1)} %upper.1, s32[256]{0:T(256)} %cell.1, s32[1,256]{1,0:T(1,128)} %bitcast.3, s32[256]{0:T(256)} %slot.1, ...), custom_call_target="tpu_custom_call" | custom-call | flops 22000000 | bytes 4700000 | tf_op jit(solution)/shard_map/sweep/pallas_call | solution.py:523
  40.6 0.8 %store.1 = (f32[5,16,2048]{2,1,0:T(8,128)}, f32[3,128]{1,0:T(4,128)}, f32[5]{0:T(128)}) custom-call(f32[5,384,128]{2,1,0:T(8,128)S(1)} %get-tuple-element.6.adj, f32[3,128]{1,0:T(4,128)S(1)} %get-tuple-element.7.shell, f32[5]{0:T(128)S(1)} %get-tuple-element.8.hinge), custom_call_target="tpu_custom_call" | custom-call | tf_op jit(solution)/shard_map/store/pallas_call | solution.py:568

commit v6 on v5

--- a/solution.py
+++ b/solution.py
@@ -18,6 +18,8 @@
 LANES = 128
 CHUNKS = CELLS // LANES
 HALF = CHUNKS // 2
+OWN = 10
+SENDS = ((0, 1, 2, 3, 4, 5, 6, 7), (12, 13, 14, 15, 8, 9, 11))
 FACES = 256
 SHELL = 128
 CAP = 16
@@ -29,19 +31,16 @@
 GROUPS = 4
 GROUP_CELLS = CELLS // GROUPS
 GROUP_CHUNKS = CHUNKS // GROUPS
-HINGE_AT = 0
-LOAD_AT = 16
-SLOT_AT = 64
-
-
-def chunk_of(dev):
-    x, y = dev // 4, dev % 4
-    return HALF * ((x + y) % 2) + 2 * x + y // 2
-
-
-def device_of(half, j):
-    x = j // 2
-    return 4 * x + 2 * (j % 2) + (half + x) % 2
+LOAD_AT = 0
+SLOT_AT = 48
+
+
+def owner_of(dev, pos):
+    return 4 * ((dev // 4 + pos // 4 + 2) % 4) + (dev + pos + 2) % 4
+
+
+def mirror(pos):
+    return 4 * ((4 - pos // 4) % 4) + (4 - pos % 4) % 4
 
 
 def split(value):
@@ -74,6 +73,9 @@
     fmap_v,
     arm_v,
     terms,
+    prefix,
+    weights,
+    gains,
     maps,
     maps_in,
     inc_out,
@@ -82,6 +84,8 @@
     msg,
     msg_in,
     rows_in,
+    zmsg,
+    zmsg_in,
     hmsg,
     hmsg_in,
     ready,
@@ -93,6 +97,8 @@
     inc_rsem,
     face_ssem,
     face_rsem,
+    z_ssem,
+    z_rsem,
     hinge_ssem,
     hinge_rsem,
 ):
@@ -101,16 +107,18 @@
     barrier = pltpu.get_barrier_semaphore()
 
     def load_copies(g):
-        cells = pl.ds(g * GROUP_CELLS, GROUP_CELLS)
+        block = (me // 4 + g + 2) % 4
+        cells = pl.ds(pl.multiple_of(block * GROUP_CELLS, GROUP_CELLS), GROUP_CELLS)
+        here = pl.ds(g * GROUP_CELLS, GROUP_CELLS)
         return (
             pltpu.make_async_copy(
-                inv_diag.at[:, :, :, cells], d_v.at[:, :, :, cells], load_sem.at[g, 0]
+                inv_diag.at[:, :, :, cells], d_v.at[:, :, :, here], load_sem.at[g, 0]
             ),
             pltpu.make_async_copy(
-                upper.at[:, :, :, cells], u_v.at[:, :, :, cells], load_sem.at[g, 1]
+                upper.at[:, :, :, cells], u_v.at[:, :, :, here], load_sem.at[g, 1]
             ),
             pltpu.make_async_copy(
-                forcing.at[:, :, cells], f_v.at[:, :, cells], load_sem.at[g, 2]
+                forcing.at[:, :, cells], f_v.at[:, :, here], load_sem.at[g, 2]
             ),
         )
 
@@ -133,9 +141,9 @@
     for copy in small:
         copy.start()
 
-    def greet_span(r, carry):
+    def greet_span(pos, carry):
         pl.semaphore_signal(
-            barrier, inc=1, device_id=((me + r) % NS, q), device_id_type=MESH
+            barrier, inc=1, device_id=(owner_of(me, pos), q), device_id_type=MESH
         )
         return carry
 
@@ -145,9 +153,10 @@
         return (me, ((depth + distance) % (NP // 2)) * 2 + (core + other) % 2)
 
     near = [along(0, 1)] + [along(d, other) for d in (1, -1) for other in (0, 1)]
+    lax.fori_loop(0, OWN, greet_span, 0)
+    lax.fori_loop(OWN + 1, NS, greet_span, 0)
     for peer in near:
         pl.semaphore_signal(barrier, inc=1, device_id=peer, device_id_type=MESH)
-    lax.fori_loop(1, NS, greet_span, 0)
 
     def tell(step):
         for d in (1 << step, -(1 << step)):
@@ -172,7 +181,9 @@
         )
 
     def chunk_terms(c, carry):
-        cells = pl.ds(pl.multiple_of(c * LANES, LANES), LANES)
+        cells = pl.ds(
+            pl.multiple_of(c // 4 * GROUP_CELLS + (me + c + 2) % 4 * LANES, LANES), LANES
+        )
         rows = pl.ds(c * TERM_PITCH, PLANES)
         up = [
             [u_v[j, m, :, cells].astype(jnp.float32) for m in range(FIELDS)]
@@ -204,8 +215,13 @@
             out.append(total if start is None else total + start[i])
         return out
 
+    def prefix_rows(half, k):
+        return pl.ds(pl.multiple_of((k * 2 + half) * HALF, HALF), HALF)
+
     def section_map(half):
         state = tuple(term(n, half, PLANES - 1) for n in range(COMPS))
+        for n in range(COMPS):
+            prefix[n, prefix_rows(half, PLANES - 1), :] = state[n]
 
         def compose(step, state):
             k = PLANES - 2 - step
@@ -217,6 +233,8 @@
                 for i in range(FIELDS):
                     new[i * FIELDS + col] = column[i]
             new[FIELDS * FIELDS :] = matvec(coupling, state[FIELDS * FIELDS :], source)
+            for n in range(COMPS):
+                prefix[n, prefix_rows(half, k), :] = new[n]
             return tuple(new)
 
         state = lax.fori_loop(0, PLANES - 1, compose, state)
@@ -242,8 +260,6 @@
     for n in range(COMPS, MAP_ROWS):
         maps[pl.ds(n, CHUNKS, stride=MAP_PITCH), :] = jnp.zeros((CHUNKS, LANES), jnp.float32)
 
-    my_chunk = chunk_of(me)
-    my_j = my_chunk % HALF
     for half in range(2):
         for g in range(half * GROUPS // 2, (half + 1) * GROUPS // 2):
             for copy in load_copies(g):
@@ -254,17 +270,8 @@
             pl.semaphore_wait(barrier, NS - 1 + len(near))
             tell(0)
 
-        def send_map(t, carry):
-            j = (my_j + t) % HALF
-            dest = device_of(half, j)
-
-            @pl.when(dest != me)
-            def _():
-                map_copy(half * HALF + j, dest, me).start()
-
-            return carry
-
-        lax.fori_loop(0, HALF, send_map, 0)
+        for pos in SENDS[half]:
+            map_copy(pos, owner_of(me, pos), me).start()
 
     hear(0)
     tell(1)
@@ -275,8 +282,9 @@
     face_plane = face_cell // CELLS
     face_at = face_cell % CELLS
     for c in range(CHUNKS):
-        at = lax.broadcasted_iota(jnp.int32, (LANES, FACES), 0) + c * LANES
-        hot[pl.ds(c * LANES, LANES), :] = jnp.where(at == face_at, 1.0, 0.0).astype(jnp.bfloat16)
+        at = lax.broadcasted_iota(jnp.int32, (LANES, FACES), 0)
+        here = face_at - owner_of(me, c) * LANES
+        hot[pl.ds(c * LANES, LANES), :] = jnp.where(at == here, 1.0, 0.0).astype(jnp.bfloat16)
     plane_hit = lax.broadcasted_iota(jnp.int32, (PLANES, FACES), 0) == face_plane
     face_id = lax.broadcasted_iota(jnp.int32, (1, FACES), 1)
     live = jnp.where(face_id < count[0], 1.0, 0.0)
@@ -300,9 +308,31 @@
     hear(1)
     tell(2)
 
+    def by_face(left, right):
+        return lax.dot_general(
+            left, right, (((1,), (1,)), ((), ())), preferred_element_type=jnp.float32
+        )
+
+    at_plane = jnp.concatenate(split(jnp.where(plane_hit, weight, 0.0)), axis=0)
+    for c in range(CHUNKS):
+        spread = by_face(at_plane, hot[pl.ds(c * LANES, LANES), :])
+        weights[pl.ds(c * TERM_PITCH, PLANES), :] = spread[:PLANES] + spread[PLANES:]
+    for half in range(2):
+
+        def add_plane(k, total):
+            weight_k = weights[pl.ds(half * HALF * TERM_PITCH + k, HALF, stride=TERM_PITCH), :]
+            return tuple(
+                total[n] + weight_k * prefix[n, prefix_rows(half, k), :] for n in range(COMPS)
+            )
+
+        zero = jnp.zeros((HALF, LANES), jnp.float32)
+        total = lax.fori_loop(0, PLANES, add_plane, (zero,) * COMPS)
+        for n in range(COMPS):
+            gains[n, pl.ds(half * HALF, HALF), :] = total[n]
+
     all_maps = everything(maps_in, (NS - 1) * MAP_ROWS, map_ssem, map_rsem, near[0])
     all_maps.wait_recv()
-    maps_in[map_rows(me), :] = maps[out_rows(my_chunk), :]
+    maps_in[map_rows(me), :] = maps[out_rows(OWN), :]
     vec = [jnp.zeros((1, LANES), jnp.float32) for _ in range(FIELDS)]
     for section in range(NS - 1, 0, -1):
 
@@ -314,24 +344,23 @@
         for i in range(FIELDS):
             inc_out[pl.ds((section - 1) * 8 + i, 1), :] = vec[i]
 
-    def inc_copy(dest, c, source):
-        return pltpu.make_async_remote_copy(
+    def send_inc(pos, carry):
+        dest = owner_of(me, pos)
+        pltpu.make_async_remote_copy(
             src_ref=inc_out.at[pl.ds(pl.multiple_of(dest * 8, 8), 8), :],
-            dst_ref=inc_in.at[pl.ds(pl.multiple_of(c * 8, 8), 8), :],
+            dst_ref=inc_in.at[pl.ds(pl.multiple_of(mirror(pos) * 8, 8), 8), :],
             send_sem=inc_ssem,
             recv_sem=inc_rsem,
             device_id=(dest, q),
             device_id_type=MESH,
-        )
-
-    def send_inc(r, carry):
-        inc_copy((me + r) % NS, my_chunk, me).start()
+        ).start()
         return carry
 
-    lax.fori_loop(1, NS, send_inc, 0)
+    lax.fori_loop(0, OWN, send_inc, 0)
+    lax.fori_loop(OWN + 1, NS, send_inc, 0)
     all_inc = everything(inc_in, (NS - 1) * 8, inc_ssem, inc_rsem, near[0])
     all_inc.wait_recv()
-    inc_in[pl.ds(pl.multiple_of(my_chunk * 8, 8), 8), :] = inc_out[
+    inc_in[pl.ds(OWN * 8, 8), :] = inc_out[
         pl.ds(pl.multiple_of(me * 8, 8), 8), :
     ]
 
@@ -339,6 +368,44 @@
         tuple(inc_in[pl.ds(half * HALF * 8 + i, HALF, stride=8), :] for i in range(FIELDS))
         for half in range(2)
     )
+
+    partial = [
+        sum(gains[FIELDS * FIELDS + i, pl.ds(half * HALF, HALF), :] for half in range(2))
+        for i in range(FIELDS)
+    ]
+    for half in range(2):
+        for i in range(FIELDS):
+            for j in range(FIELDS):
+                gain = gains[i * FIELDS + j, pl.ds(half * HALF, HALF), :]
+                partial[i] = partial[i] + gain * start[half][j]
+    columns = jnp.concatenate(
+        [jnp.sum(partial[i], axis=0, keepdims=True) for i in range(FIELDS)]
+        + [jnp.zeros((8 - FIELDS, LANES), jnp.float32)],
+        axis=0,
+    )
+    diagonal = lax.broadcasted_iota(jnp.int32, (8, LANES), 0) == lax.broadcasted_iota(
+        jnp.int32, (8, LANES), 1
+    )
+    hmsg[0] = jnp.sum(
+        jnp.where(diagonal, jnp.sum(columns, axis=1, keepdims=True), 0.0), axis=0, keepdims=True
+    )
+
+    def hinge_copy(dest, source):
+        return pltpu.make_async_remote_copy(
+            src_ref=hmsg.at[0],
+            dst_ref=hmsg_in.at[source],
+            send_sem=hinge_ssem,
+            recv_sem=hinge_rsem,
+            device_id=(dest, q),
+            device_id_type=MESH,
+        )
+
+    def send_hinge(pos, carry):
+        hinge_copy(owner_of(me, pos), me).start()
+        return carry
+
+    lax.fori_loop(0, OWN, send_hinge, 0)
+    lax.fori_loop(OWN + 1, NS, send_hinge, 0)
 
     def sweep(step, states):
         k = PLANES - 1 - step
@@ -381,29 +448,15 @@
         for i in range(1, FIELDS):
             total = total + fmap_v[i, pl.ds(a, 1), :] * rows[i]
         load_rows.append(rank_hot * (total * live))
-    hinge_rows = jnp.concatenate(
-        [rows[i] * weight for i in range(FIELDS)]
-        + [jnp.zeros((LANES - FIELDS, FACES), jnp.float32)],
-        axis=0,
-    )
     face_rows = jnp.concatenate(
-        [jnp.zeros((LOAD_AT, FACES), jnp.float32)]
-        + load_rows
+        load_rows
         + [slot_rows, jnp.zeros((LANES - SLOT_AT - CAP, FACES), jnp.float32)],
         axis=0,
     )
 
-    def by_face(left, right):
-        return lax.dot_general(
-            left, right, (((1,), (1,)), ((), ())), preferred_element_type=jnp.float32
-        )
-
-    every = jnp.ones((NP, FACES), jnp.bfloat16)
     packed = jnp.zeros((NP, LANES), jnp.float32)
     for piece in split(face_rows):
         packed = packed + by_face(owner_hot16, piece)
-    for piece in split(hinge_rows):
-        packed = packed + by_face(every, piece)
     msg[:, 0, :] = packed
 
     def face_copy(dest, source):
@@ -418,35 +471,37 @@
 
     hear(2)
 
-    def send_face(r, carry):
-        face_copy((q + r) % NP, q).start()
+    def far_first(t):
+        return (q + NP // 2 + (t + 1) // 2 * (1 - 2 * (t % 2))) % NP
+
+    def send_face(t, carry):
+        face_copy(far_first(t), q).start()
         return carry
 
-    lax.fori_loop(1, NP, send_face, 0)
+    lax.fori_loop(0, NP - 1, send_face, 0)
+    all_hinge = everything(hmsg_in, NS - 1, hinge_ssem, hinge_rsem, near[0])
+    all_hinge.wait_recv()
+    hmsg_in[me] = hmsg[0]
+    zmsg[0] = jnp.sum(hmsg_in[...], axis=0)
+
+    def send_z(t, carry):
+        pltpu.make_async_remote_copy(
+            src_ref=zmsg.at[0],
+            dst_ref=zmsg_in.at[q],
+            send_sem=z_ssem,
+            recv_sem=z_rsem,
+            device_id=(me, far_first(t)),
+            device_id_type=MESH,
+        ).start()
+        return carry
+
+    lax.fori_loop(0, NP - 1, send_z, 0)
     all_faces = everything(msg_in, NP - 1, face_ssem, face_rsem, near[0])
     all_faces.wait_recv()
     msg_in[q] = msg[q]
     for peer in range(NP):
         rows_in[pl.ds(peer, 1), :] = msg_in[peer]
     arrived = rows_in[...]
-
-    hmsg[0] = jnp.sum(arrived, axis=0, keepdims=True)
-
-    def hinge_copy(dest, source):
-        return pltpu.make_async_remote_copy(
-            src_ref=hmsg.at[0],
-            dst_ref=hmsg_in.at[source],
-            send_sem=hinge_ssem,
-            recv_sem=hinge_rsem,
-            device_id=(dest, q),
-            device_id_type=MESH,
-        )
-
-    def send_hinge(r, carry):
-        hinge_copy((me + r) % NS, me).start()
-        return carry
-
-    lax.fori_loop(1, NS, send_hinge, 0)
 
     lane = lax.broadcasted_iota(jnp.int32, (NP, LANES), 1) + 1
     loads = [jnp.zeros((NP, SHELL), jnp.float32) for _ in range(LOADS)]
@@ -462,19 +517,22 @@
     all_maps.wait_send()
     all_inc.wait_send()
     all_faces.wait_send()
-    all_hinge = everything(hmsg_in, NS - 1, hinge_ssem, hinge_rsem, near[0])
     all_hinge.wait_send()
-    all_hinge.wait_recv()
-    hmsg_in[me] = hmsg[0]
-    total = jnp.sum(hmsg_in[:, 0, :], axis=0) * (1.0 / math.sqrt(NS * NP * FACES))
+    all_z = everything(zmsg_in, NP - 1, z_ssem, z_rsem, near[0])
+    all_z.wait_send()
+    all_z.wait_recv()
+    zmsg_in[q] = zmsg[0]
+    total = jnp.sum(zmsg_in[:, 0, :], axis=0) * (1.0 / math.sqrt(NS * NP * FACES))
     hinge_out[...] = total[:FIELDS]
 
 
 def store(adj, shell, hinge, adj_out, shell_out, hinge_out, adj_sem, shell_sem, hinge_sem):
+    me = lax.axis_index("span")
     for c in range(CHUNKS):
+        cells = pl.ds(pl.multiple_of(owner_of(me, c) * LANES, LANES), LANES)
         pltpu.make_async_copy(
             adj.at[:, pl.ds(c * ADJ_PITCH, PLANES), :],
-            adj_out.at[:, :, pl.ds(c * LANES, LANES)],
+            adj_out.at[:, :, cells],
             adj_sem,
         ).start()
     rest = (
@@ -542,6 +600,9 @@
             pltpu.VMEM((FIELDS, LOADS, FACES), f32),
             pltpu.VMEM((FACES,), f32),
             pltpu.VMEM((COMPS, CHUNKS * TERM_PITCH, LANES), f32),
+            pltpu.VMEM((COMPS, 2 * PLANES * HALF, LANES), f32),
+            pltpu.VMEM((CHUNKS * TERM_PITCH, LANES), f32),
+            pltpu.VMEM((COMPS, 2 * HALF, LANES), f32),
             pltpu.VMEM((CHUNKS * MAP_PITCH, LANES), f32),
             pltpu.VMEM((NS * MAP_ROWS, LANES), f32),
             pltpu.VMEM((NS * 8, LANES), f32),
@@ -551,12 +612,14 @@
             pltpu.VMEM((NP, 1, LANES), f32),
             pltpu.VMEM((NP, LANES), f32),
             pltpu.VMEM((1, 1, LANES), f32),
+            pltpu.VMEM((NP, 1, LANES), f32),
+            pltpu.VMEM((1, 1, LANES), f32),
             pltpu.VMEM((NS, 1, LANES), f32),
             pltpu.SemaphoreType.REGULAR((3,)),
             dma((GROUPS, 3)),
             dma((6,)),
         ]
-        + [dma] * 8,
+        + [dma] * 10,
         compiler_params=pltpu.CompilerParams(
             collective_id=0, has_side_effects=True, vmem_limit_bytes=40 * 1024 * 1024
         ),

time: 41.6 us -> 40.9 us (0.983)
  Pallas kernels: 40.2 us -> 39.5 us
    pallas_call x1, Pallas kernels: 39.3 us -> 38.6 us  [on_device(): pl.pallas_call(kernel, out_shape=(pltpu.VMEM((FIELDS, CHUNKS * ADJ_PITCH,...]
where the time goes in v6:
time: 40.9 us; the launch traced here: 40.8 us
  Pallas kernels  39.5 us (97%)
  between operations  1.29 us (3%)
    pallas_call x1, Pallas kernels, on_device(): pl.pallas_call(kernel, out_shape=(pltpu.VMEM((FIELDS, CHUNKS * ADJ_PITCH,...  38.6 us
    pallas_call x1, Pallas kernels, on_device(): pl.pallas_call(store, out_shape=(jax.ShapeDtypeStruct((FIELDS, PLANES, CE...  0.87 us

profile of v6, /device:TPU:1, one launch (start us, length us, event | category | flops | bytes accessed | tf_op | source)
XLA Modules:
  0.0 40.8 jit_solution(11131185181337028503)
XLA Ops:
  1.3 38.6 %sweep.1 = (f32[5,384,128]{2,1,0:T(8,128)S(1)}, f32[3,128]{1,0:T(4,128)S(1)}, f32[5]{0:T(128)S(1)}) custom-call(f32[5,16,2048]{2,1,0:T(8,128)} %forcing.1, bf16[5,5,16,2048]{3,2,1,0:T(8,128)(2,1)} %inv_diag.1, bf16[5,5,16,2048]{3,2,1,0:T(8,128)(2,1)} %upper.1, s32[256]{0:T(256)} %cell.1, s32[1,256]{1,0:T(1,128)} %bitcast.3, s32[256]{0:T(256)} %slot.1, ...), custom_call_target="tpu_custom_call" | custom-call | flops 22000000 | bytes 4700000 | tf_op jit(solution)/shard_map/sweep/pallas_call | solution.py:581
  39.9 0.9 %store.1 = (f32[5,16,2048]{2,1,0:T(8,128)}, f32[3,128]{1,0:T(4,128)}, f32[5]{0:T(128)}) custom-call(f32[5,384,128]{2,1,0:T(8,128)S(1)} %get-tuple-element.6.adj, f32[3,128]{1,0:T(4,128)S(1)} %get-tuple-element.7.shell, f32[5]{0:T(128)S(1)} %get-tuple-element.8.hinge), custom_call_target="tpu_custom_call" | custom-call | tf_op jit(solution)/shard_map/store/pallas_call | solution.py:631

commit v7 on v6

--- a/solution.py
+++ b/solution.py
@@ -76,6 +76,7 @@
     prefix,
     weights,
     gains,
+    gains_in,
     maps,
     maps_in,
     inc_out,
@@ -93,6 +94,8 @@
     small_sem,
     map_ssem,
     map_rsem,
+    gain_ssem,
+    gain_rsem,
     inc_ssem,
     inc_rsem,
     face_ssem,
@@ -264,7 +267,7 @@
         for g in range(half * GROUPS // 2, (half + 1) * GROUPS // 2):
             for copy in load_copies(g):
                 copy.wait()
-            lax.fori_loop(g * GROUP_CHUNKS, (g + 1) * GROUP_CHUNKS, chunk_terms, 0)
+            lax.fori_loop(g * GROUP_CHUNKS, (g + 1) * GROUP_CHUNKS, chunk_terms, 0, unroll=2)
         section_map(half)
         if half == 0:
             pl.semaphore_wait(barrier, NS - 1 + len(near))
@@ -317,6 +320,9 @@
     for c in range(CHUNKS):
         spread = by_face(at_plane, hot[pl.ds(c * LANES, LANES), :])
         weights[pl.ds(c * TERM_PITCH, PLANES), :] = spread[:PLANES] + spread[PLANES:]
+    constant = [jnp.zeros((HALF, LANES), jnp.float32) for _ in range(FIELDS)]
+    for n in range(FIELDS * FIELDS, MAP_ROWS):
+        gains[pl.ds(n, CHUNKS, stride=MAP_PITCH), :] = jnp.zeros((CHUNKS, LANES), jnp.float32)
     for half in range(2):
 
         def add_plane(k, total):
@@ -327,8 +333,19 @@
 
         zero = jnp.zeros((HALF, LANES), jnp.float32)
         total = lax.fori_loop(0, PLANES, add_plane, (zero,) * COMPS)
-        for n in range(COMPS):
-            gains[n, pl.ds(half * HALF, HALF), :] = total[n]
+        for n in range(FIELDS * FIELDS):
+            gains[pl.ds(half * HALF * MAP_PITCH + n, HALF, stride=MAP_PITCH), :] = total[n]
+        constant = [constant[i] + total[FIELDS * FIELDS + i] for i in range(FIELDS)]
+        for pos in SENDS[half]:
+            dest = owner_of(me, pos)
+            pltpu.make_async_remote_copy(
+                src_ref=gains.at[out_rows(pos), :],
+                dst_ref=gains_in.at[map_rows(me), :],
+                send_sem=gain_ssem,
+                recv_sem=gain_rsem,
+                device_id=(dest, q),
+                device_id_type=MESH,
+            ).start()
 
     all_maps = everything(maps_in, (NS - 1) * MAP_ROWS, map_ssem, map_rsem, near[0])
     all_maps.wait_recv()
@@ -358,26 +375,16 @@
 
     lax.fori_loop(0, OWN, send_inc, 0)
     lax.fori_loop(OWN + 1, NS, send_inc, 0)
-    all_inc = everything(inc_in, (NS - 1) * 8, inc_ssem, inc_rsem, near[0])
-    all_inc.wait_recv()
-    inc_in[pl.ds(OWN * 8, 8), :] = inc_out[
-        pl.ds(pl.multiple_of(me * 8, 8), 8), :
-    ]
-
-    start = tuple(
-        tuple(inc_in[pl.ds(half * HALF * 8 + i, HALF, stride=8), :] for i in range(FIELDS))
-        for half in range(2)
-    )
-
-    partial = [
-        sum(gains[FIELDS * FIELDS + i, pl.ds(half * HALF, HALF), :] for half in range(2))
-        for i in range(FIELDS)
-    ]
-    for half in range(2):
-        for i in range(FIELDS):
-            for j in range(FIELDS):
-                gain = gains[i * FIELDS + j, pl.ds(half * HALF, HALF), :]
-                partial[i] = partial[i] + gain * start[half][j]
+    all_gains = everything(gains_in, (NS - 1) * MAP_ROWS, gain_ssem, gain_rsem, near[0])
+    all_gains.wait_recv()
+    gains_in[map_rows(me), :] = gains[out_rows(OWN), :]
+    partial = constant
+    for section in range(NS - 1):
+        entering = inc_out[pl.ds(section * 8, 8), :]
+        partial = [
+            partial[i] + gains_in[pl.ds(section * MAP_ROWS + i * FIELDS, 8), :] * entering
+            for i in range(FIELDS)
+        ]
     columns = jnp.concatenate(
         [jnp.sum(partial[i], axis=0, keepdims=True) for i in range(FIELDS)]
         + [jnp.zeros((8 - FIELDS, LANES), jnp.float32)],
@@ -406,6 +413,17 @@
 
     lax.fori_loop(0, OWN, send_hinge, 0)
     lax.fori_loop(OWN + 1, NS, send_hinge, 0)
+
+    all_inc = everything(inc_in, (NS - 1) * 8, inc_ssem, inc_rsem, near[0])
+    all_inc.wait_recv()
+    inc_in[pl.ds(OWN * 8, 8), :] = inc_out[
+        pl.ds(pl.multiple_of(me * 8, 8), 8), :
+    ]
+
+    start = tuple(
+        tuple(inc_in[pl.ds(half * HALF * 8 + i, HALF, stride=8), :] for i in range(FIELDS))
+        for half in range(2)
+    )
 
     def sweep(step, states):
         k = PLANES - 1 - step
@@ -515,6 +533,7 @@
         shell_out[pl.ds(a, 1), :] = jnp.sum(loads[a], axis=0, keepdims=True)
 
     all_maps.wait_send()
+    all_gains.wait_send()
     all_inc.wait_send()
     all_faces.wait_send()
     all_hinge.wait_send()
@@ -602,7 +621,8 @@
             pltpu.VMEM((COMPS, CHUNKS * TERM_PITCH, LANES), f32),
             pltpu.VMEM((COMPS, 2 * PLANES * HALF, LANES), f32),
             pltpu.VMEM((CHUNKS * TERM_PITCH, LANES), f32),
-            pltpu.VMEM((COMPS, 2 * HALF, LANES), f32),
+            pltpu.VMEM((CHUNKS * MAP_PITCH, LANES), f32),
+            pltpu.VMEM((NS * MAP_ROWS, LANES), f32),
             pltpu.VMEM((CHUNKS * MAP_PITCH, LANES), f32),
             pltpu.VMEM((NS * MAP_ROWS, LANES), f32),
             pltpu.VMEM((NS * 8, LANES), f32),
@@ -619,7 +639,7 @@
             dma((GROUPS, 3)),
             dma((6,)),
         ]
-        + [dma] * 10,
+        + [dma] * 12,
         compiler_params=pltpu.CompilerParams(
             collective_id=0, has_side_effects=True, vmem_limit_bytes=40 * 1024 * 1024
         ),

time: 40.9 us -> 39.5 us (0.966)
  Pallas kernels: 39.5 us -> 38.1 us
    pallas_call x1, Pallas kernels: 38.6 us -> 37.2 us  [on_device(): pl.pallas_call(kernel, out_shape=(pltpu.VMEM((FIELDS, CHUNKS * ADJ_PITCH,...]
where the time goes in v7:
time: 39.5 us; the launch traced here: 39.4 us
  Pallas kernels  38.1 us (96%)
  between operations  1.29 us (3%)
    pallas_call x1, Pallas kernels, on_device(): pl.pallas_call(kernel, out_shape=(pltpu.VMEM((FIELDS, CHUNKS * ADJ_PITCH,...  37.2 us
    pallas_call x1, Pallas kernels, on_device(): pl.pallas_call(store, out_shape=(jax.ShapeDtypeStruct((FIELDS, PLANES, CE...  0.87 us

profile of v7, /device:TPU:1, one launch (start us, length us, event | category | flops | bytes accessed | tf_op | source)
XLA Modules:
  0.0 39.4 jit_solution(16509853420136289943)
XLA Ops:
  1.3 37.2 %sweep.1 = (f32[5,384,128]{2,1,0:T(8,128)S(1)}, f32[3,128]{1,0:T(4,128)S(1)}, f32[5]{0:T(128)S(1)}) custom-call(f32[5,16,2048]{2,1,0:T(8,128)} %forcing.1, bf16[5,5,16,2048]{3,2,1,0:T(8,128)(2,1)} %inv_diag.1, bf16[5,5,16,2048]{3,2,1,0:T(8,128)(2,1)} %upper.1, s32[256]{0:T(256)} %cell.1, s32[1,256]{1,0:T(1,128)} %bitcast.3, s32[256]{0:T(256)} %slot.1, ...), custom_call_target="tpu_custom_call" | custom-call | flops 22000000 | bytes 4700000 | tf_op jit(solution)/shard_map/sweep/pallas_call | solution.py:600
  38.5 0.9 %store.1 = (f32[5,16,2048]{2,1,0:T(8,128)}, f32[3,128]{1,0:T(4,128)}, f32[5]{0:T(128)}) custom-call(f32[5,384,128]{2,1,0:T(8,128)S(1)} %get-tuple-element.6.adj, f32[3,128]{1,0:T(4,128)S(1)} %get-tuple-element.7.shell, f32[5]{0:T(128)S(1)} %get-tuple-element.8.hinge), custom_call_target="tpu_custom_call" | custom-call | tf_op jit(solution)/shard_map/store/pallas_call | solution.py:651

commit v8 on v7

--- a/solution.py
+++ b/solution.py
@@ -332,20 +332,23 @@
             )
 
         zero = jnp.zeros((HALF, LANES), jnp.float32)
-        total = lax.fori_loop(0, PLANES, add_plane, (zero,) * COMPS)
+        total = lax.fori_loop(0, PLANES, add_plane, (zero,) * COMPS, unroll=4)
         for n in range(FIELDS * FIELDS):
             gains[pl.ds(half * HALF * MAP_PITCH + n, HALF, stride=MAP_PITCH), :] = total[n]
         constant = [constant[i] + total[FIELDS * FIELDS + i] for i in range(FIELDS)]
-        for pos in SENDS[half]:
-            dest = owner_of(me, pos)
-            pltpu.make_async_remote_copy(
-                src_ref=gains.at[out_rows(pos), :],
-                dst_ref=gains_in.at[map_rows(me), :],
-                send_sem=gain_ssem,
-                recv_sem=gain_rsem,
-                device_id=(dest, q),
-                device_id_type=MESH,
-            ).start()
+
+        @pl.when(me != NS - 1)
+        def _():
+            for pos in SENDS[half]:
+                dest = owner_of(me, pos)
+                pltpu.make_async_remote_copy(
+                    src_ref=gains.at[out_rows(pos), :],
+                    dst_ref=gains_in.at[map_rows(me), :],
+                    send_sem=gain_ssem,
+                    recv_sem=gain_rsem,
+                    device_id=(dest, q),
+                    device_id_type=MESH,
+                ).start()
 
     all_maps = everything(maps_in, (NS - 1) * MAP_ROWS, map_ssem, map_rsem, near[0])
     all_maps.wait_recv()
@@ -376,7 +379,15 @@
     lax.fori_loop(0, OWN, send_inc, 0)
     lax.fori_loop(OWN + 1, NS, send_inc, 0)
     all_gains = everything(gains_in, (NS - 1) * MAP_ROWS, gain_ssem, gain_rsem, near[0])
-    all_gains.wait_recv()
+
+    @pl.when(me == NS - 1)
+    def _():
+        all_gains.wait_recv()
+
+    @pl.when(me != NS - 1)
+    def _():
+        everything(gains_in, (NS - 2) * MAP_ROWS, gain_ssem, gain_rsem, near[0]).wait_recv()
+
     gains_in[map_rows(me), :] = gains[out_rows(OWN), :]
     partial = constant
     for section in range(NS - 1):
@@ -533,7 +544,11 @@
         shell_out[pl.ds(a, 1), :] = jnp.sum(loads[a], axis=0, keepdims=True)
 
     all_maps.wait_send()
-    all_gains.wait_send()
+
+    @pl.when(me != NS - 1)
+    def _():
+        all_gains.wait_send()
+
     all_inc.wait_send()
     all_faces.wait_send()
     all_hinge.wait_send()

time: 39.5 us -> 39.5 us (level)
  no operation moved by 1% of the time
where the time goes in v8:
time: 39.5 us; the launch traced here: 39.3 us
  Pallas kernels  38 us (96%)
  between operations  1.29 us (3%)
    pallas_call x1, Pallas kernels, on_device(): pl.pallas_call(kernel, out_shape=(pltpu.VMEM((FIELDS, CHUNKS * ADJ_PITCH,...  37.2 us
    pallas_call x1, Pallas kernels, on_device(): pl.pallas_call(store, out_shape=(jax.ShapeDtypeStruct((FIELDS, PLANES, CE...  0.87 us

profile of v8, /device:TPU:1, one launch (start us, length us, event | category | flops | bytes accessed | tf_op | source)
XLA Modules:
  0.0 39.3 jit_solution(13700837570996726876)
XLA Ops:
  1.3 37.2 %sweep.1 = (f32[5,384,128]{2,1,0:T(8,128)S(1)}, f32[3,128]{1,0:T(4,128)S(1)}, f32[5]{0:T(128)S(1)}) custom-call(f32[5,16,2048]{2,1,0:T(8,128)} %forcing.1, bf16[5,5,16,2048]{3,2,1,0:T(8,128)(2,1)} %inv_diag.1, bf16[5,5,16,2048]{3,2,1,0:T(8,128)(2,1)} %upper.1, s32[256]{0:T(256)} %cell.1, s32[1,256]{1,0:T(1,128)} %bitcast.3, s32[256]{0:T(256)} %slot.1, ...), custom_call_target="tpu_custom_call" | custom-call | flops 22000000 | bytes 4700000 | tf_op jit(solution)/shard_map/sweep/pallas_call | solution.py:615
  38.5 0.9 %store.1 = (f32[5,16,2048]{2,1,0:T(8,128)}, f32[3,128]{1,0:T(4,128)}, f32[5]{0:T(128)}) custom-call(f32[5,384,128]{2,1,0:T(8,128)S(1)} %get-tuple-element.6.adj, f32[3,128]{1,0:T(4,128)S(1)} %get-tuple-element.7.shell, f32[5]{0:T(128)S(1)} %get-tuple-element.8.hinge), custom_call_target="tpu_custom_call" | custom-call | tf_op jit(solution)/shard_map/store/pallas_call | solution.py:666
